TPU v7x, 32 devices: a whole 2x2x4 slice. The times are simulated.
32 devices in a mesh: group: 2 (over y), det: 4 (over z), tm: 2 (over x), pol: 2 (over core).
Axes of the slice: x: 2, y: 2, z: 4, core: 2. Of those that a mesh axis runs over, the one named last changes fastest.
Arguments:
- timestream: bfloat16 [128, 16384], P(('group', 'det', 'pol'), 'tm'), parts along dimension 0, may hold values from -6 to 6
- hwp_index: int32 [32768], P(('group', 'tm')), parts along dimension 0, may hold values from 0 to 8191
- flags: int32 [128, 16384], P(('group', 'det', 'pol'), 'tm'), parts along dimension 0, may hold values 0 or 1
- pixel_index: int32 [128, 16384], P(('group', 'det', 'pol'), 'tm'), parts along dimension 0, may hold values from 0 to 16383, as said below
- tile_index: int32 [128, 32], P(('group', 'det', 'pol'), 'tm'), parts along dimension 0, may hold values from 0 to 15
- wafer: int32 [128], P(('group', 'det', 'pol')), parts along dimension 0, may hold values from 0 to 6
- taps: float32 [7, 33], replicated, may hold values from -1 to 1
- detector_angle: float32 [128], P(('group', 'det', 'pol')), parts along dimension 0, may hold values from -3.140625 to 3.140625
Outputs:
- e_modes: float32 [2, 1024, 512], P(None, ('group', 'det', 'tm', 'pol')), parts along dimension 1
- b_modes: float32 [2, 1024, 512], P(None, ('group', 'det', 'tm', 'pol')), parts along dimension 1
There are 2 independent parts, one for each index of `group`. A program takes and returns all parts, laid end to end along the dimension named above; an argument that names none is the same for every part. Nothing has to cross between parts.
Inputs may be any that keep to these rules, and one draw needn't show every extreme that they name: `pixel_index`: position inside a tile, row-major; in each pointing block of 512 samples of one detector, exactly 128 samples lie in each band of 32 consecutive tile rows.
All inputs are finite; a program needn't handle non-finite values. No bound on the sum of `flags` on one device may be relied on, other than what follows from the above.
Results may differ from a plain program's by a relative error of at most 0.0029.
Values may be sent and summed in bfloat16 or wider, within the bound.
A program may use at most 64 MiB of HBM per device.

v0:
```python
import math

import jax
import jax.numpy as jnp
from jax import lax
from jax.sharding import PartitionSpec as P

TILE = 128
MAPY = 2048
KY = 512
NANG = 8192


HIGH = lax.Precision.HIGHEST


def extended(block, sides, width):
    for axis, dim in sides:
        count = lax.axis_size(axis)
        forward = [(i, i + 1) for i in range(count - 1)]
        backward = [(target, source) for source, target in forward]
        low = lax.ppermute(
            lax.slice_in_dim(block, block.shape[dim] - width, None, axis=dim), axis, forward
        )
        high = lax.ppermute(lax.slice_in_dim(block, 0, width, axis=dim), axis, backward)
        block = jnp.concatenate([low, block, high], axis=dim)
    return block


def transform_rows(strip_map):
    y_pos = jnp.arange(MAPY, dtype=jnp.int32)[:, None]
    ky_pos = jnp.arange(KY, dtype=jnp.int32)[None, :]
    angles = (y_pos * ky_pos % MAPY).astype(jnp.float32) * (2.0 * math.pi / MAPY)
    real_part = jnp.einsum("cry,yk->ckr", strip_map, jnp.cos(angles), precision=HIGH)
    imag_part = -jnp.einsum("cry,yk->ckr", strip_map, jnp.sin(angles), precision=HIGH)
    return jnp.stack([real_part, imag_part], axis=1)


def twiddle_table(first, second, length):
    return (first * second % length).astype(jnp.float32) * (2.0 * math.pi / length)


def transform_columns(real_in, imag_in):
    lead, kept, length = real_in.shape
    outer = TILE
    inner = length // outer
    real_grid = real_in.reshape(lead, kept, outer, inner)
    imag_grid = imag_in.reshape(lead, kept, outer, inner)
    outer_pos = jnp.arange(outer, dtype=jnp.int32)
    inner_pos = jnp.arange(inner, dtype=jnp.int32)
    first_angle = twiddle_table(outer_pos[:, None], outer_pos[None, :], outer)
    first_cos = jnp.cos(first_angle)
    first_sin = jnp.sin(first_angle)
    section_real = jnp.einsum("ckab,ad->ckdb", real_grid, first_cos, precision=HIGH) + jnp.einsum(
        "ckab,ad->ckdb", imag_grid, first_sin, precision=HIGH
    )
    section_imag = jnp.einsum("ckab,ad->ckdb", imag_grid, first_cos, precision=HIGH) - jnp.einsum(
        "ckab,ad->ckdb", real_grid, first_sin, precision=HIGH
    )
    mid_angle = twiddle_table(outer_pos[:, None], inner_pos[None, :], length)
    mid_cos = jnp.cos(mid_angle)
    mid_sin = jnp.sin(mid_angle)
    turned_real = section_real * mid_cos + section_imag * mid_sin
    turned_imag = section_imag * mid_cos - section_real * mid_sin
    last_angle = twiddle_table(inner_pos[:, None], inner_pos[None, :], inner)
    last_cos = jnp.cos(last_angle)
    last_sin = jnp.sin(last_angle)
    final_real = jnp.einsum("ckdb,be->cked", turned_real, last_cos, precision=HIGH) + jnp.einsum(
        "ckdb,be->cked", turned_imag, last_sin, precision=HIGH
    )
    final_imag = jnp.einsum("ckdb,be->cked", turned_imag, last_cos, precision=HIGH) - jnp.einsum(
        "ckdb,be->cked", turned_real, last_sin, precision=HIGH
    )
    return (final_real.reshape(lead, kept, length), final_imag.reshape(lead, kept, length))


def body(timestream, hwp_index, flags, pixel_index, tile_index, wafer, taps, detector_angle):
    det_rows, time_len = timestream.shape
    tap_count = taps.shape[1]
    rim_width = (tap_count - 1) // 2
    padded = extended(timestream, (("tm", 1),), rim_width)
    wafer_hot = (wafer[:, None] == jnp.arange(taps.shape[0], dtype=jnp.int32)[None, :]).astype(
        jnp.float32
    )
    det_taps = jnp.dot(wafer_hot, taps, precision=HIGH)
    filtered = jnp.zeros((det_rows, time_len), jnp.float32)
    for offset in range(tap_count):
        filtered = filtered + det_taps[:, offset : offset + 1] * padded[
            :, offset : offset + time_len
        ].astype(jnp.float32)
    hwp_turns = (4 * hwp_index % NANG).astype(jnp.float32) * (2.0 * math.pi / NANG)
    demod_phase = hwp_turns[None, :] - 2.0 * detector_angle[:, None]
    flagged = filtered * flags.astype(jnp.float32)
    q_values = (flagged * jnp.cos(demod_phase)).astype(jnp.bfloat16)
    u_values = (flagged * jnp.sin(demod_phase)).astype(jnp.bfloat16)
    block_count = tile_index.shape[1]
    block_len = time_len // block_count
    total_blocks = det_rows * block_count
    tile_cols = MAPY // TILE
    side_pos = jnp.arange(TILE, dtype=jnp.int32)
    zero_value = jnp.zeros((), jnp.bfloat16)
    batch = math.gcd(total_blocks, 16)
    rounds = total_blocks // batch
    q_blocks = q_values.reshape(rounds, batch, block_len)
    u_blocks = u_values.reshape(rounds, batch, block_len)
    pix_blocks = pixel_index.reshape(rounds, batch, block_len)

    def bin_step(band_map, inputs):
        q_part, u_part, pix_part, tile_part = inputs
        row_hot = (pix_part // TILE)[:, None, :] == side_pos[None, :, None]
        weighted = jnp.concatenate(
            [
                jnp.where(row_hot, q_part[:, None, :], zero_value),
                jnp.where(row_hot, u_part[:, None, :], zero_value),
            ],
            axis=1,
        )
        col_hot = ((pix_part % TILE)[:, :, None] == side_pos[None, None, :]).astype(jnp.bfloat16)
        tile_sums = jnp.einsum(
            "gab,gbc->gac", weighted, col_hot, preferred_element_type=jnp.float32
        )
        tile_sums = jnp.transpose(tile_sums.reshape(batch, 2, TILE, TILE), (1, 2, 0, 3))
        band_map = band_map.at[:, :, tile_part, :].add(tile_sums)
        return (band_map, None)

    band_start = jnp.zeros((2, TILE, tile_cols, TILE), jnp.float32)
    band_map, _ = lax.scan(bin_step, band_start, (q_blocks, u_blocks, pix_blocks, tile_index))
    partial_map = band_map.reshape(2, TILE, MAPY)
    owned_rows = lax.psum_scatter(partial_map, "det", scatter_dimension=1, tiled=True)
    spectrum = transform_rows(owned_rows)
    columns = lax.all_to_all(
        lax.all_to_all(spectrum, "det", split_axis=2, concat_axis=3, tiled=True),
        ("tm", "pol"),
        split_axis=2,
        concat_axis=3,
        tiled=True,
    )
    length = columns.shape[3]
    kept_now = columns.shape[2]
    final_real, final_imag = transform_columns(columns[:, 0], columns[:, 1])
    norm_scale = 1.0 / math.sqrt(length * MAPY)
    final_real = final_real * norm_scale
    final_imag = final_imag * norm_scale
    position = (lax.axis_index("det") * lax.axis_size("tm") + lax.axis_index("tm")) * lax.axis_size(
        "pol"
    ) + lax.axis_index("pol")
    kx_pos = jnp.arange(length, dtype=jnp.int32)
    freq_x = jnp.where(kx_pos < length // 2, kx_pos, kx_pos - length).astype(jnp.float32)[None, :]
    freq_y = (position * kept_now + jnp.arange(kept_now, dtype=jnp.int32)).astype(jnp.float32)[
        :, None
    ]
    radius = jnp.maximum(freq_x * freq_x + freq_y * freq_y, 1.0)
    cosine = (freq_x * freq_x - freq_y * freq_y) / radius
    sine = 2.0 * freq_x * freq_y / radius
    e_real = cosine * final_real[0] + sine * final_real[1]
    e_imag = cosine * final_imag[0] + sine * final_imag[1]
    b_real = cosine * final_real[1] - sine * final_real[0]
    b_imag = cosine * final_imag[1] - sine * final_imag[0]
    return (jnp.stack([e_real, e_imag]), jnp.stack([b_real, b_imag]))


def solution(mesh):
    in_specs = (
        P(("group", "det", "pol"), "tm"),
        P(("group", "tm")),
        P(("group", "det", "pol"), "tm"),
        P(("group", "det", "pol"), "tm"),
        P(("group", "det", "pol"), "tm"),
        P(("group", "det", "pol")),
        P(),
        P(("group", "det", "pol")),
    )
    out_specs = (
        P(None, ("group", "det", "tm", "pol"), None),
        P(None, ("group", "det", "tm", "pol"), None),
    )
    return jax.shard_map(body, mesh=mesh, in_specs=in_specs, out_specs=out_specs, check_vma=False)
```

profile of v0, /device:TPU:0, one launch (start us, length us, event | category | flops | bytes accessed | tf_op | source)
XLA Modules:
  0.0 285.7 jit_solution(703501901690124681)
XLA Ops:
  7.2 0.8 fusion.158
  8.0 1.3 collective-permute-start.1
  9.3 4.8 %collective-permute-start = (bf16[8,16]{1,0:T(8,128)(2,1)S(1)}, bf16[8,16]{1,0:T(8,128)(2,1)S(1)}, u32[]{:S(2)}, u32[]{:S(2)}) collective-permute-start(bf16[8,16]{1,0:T(8,128)(2,1)S(1)} %get-tuple-element.195), channel_id=1, source_target_pairs={{0,2},{1,3},{4,6},{5,7},{8,10},{9,11},{12,14},{13,15},{16,18},{17,... | collective-permute-start | bytes 776 | tf_op jit(solution)/shard_map/ppermute | solution.py:22
  14.1 0.8 fusion.91
  15.9 0.9 constant_dynamic-update-slice_fusion.1
  16.8 0.8 fusion.84
  17.6 0.7 broadcast_multiply_fusion
  18.2 1.1 copy.108
  19.4 5.6 %fusion.47 = (bf16[8,8192]{1,0:T(8,128)(2,1)S(1)}, f32[8,8192]{1,0:T(8,128)S(1)}) fusion(f32[8]{0:T(128)S(1)} %broadcast_multiply_fusion, f32[8192]{0:T(1024)S(1)} %fusion.84, s32[8,8192]{1,0:T(8,128)} %param.12, bf16[8,8208]{1,0:T(8,128)(2,1)S(1)} %constant_dynamic-update-slice_fusion, f32[8]{0:T(128)S(1)} %get-tuple-element.131, ...), kind=kLoop, calls=%fused_computation.76 | loop fusion | flops 9895936 | bytes 2917696 | tf_op jit(solution)/shard_map/convert_element_type | solution.py:95
  24.9 0.9 fusion.45
  26.2 85.0 %while.14 = (s32[]{:T(128)}, f32[2,128,16,128]{3,1,2,0:T(8,128)S(1)}, s32[8,16]{1,0:T(8,128)}, s32[8,16,512]{2,1,0:T(8,128)S(1)}, bf16[8,16,512]{2,1,0:T(8,128)(...) while((s32[]{:T(128)}, f32[2,128,16,128]{3,1,2,0:T(8,128)S(1)}, ...), condition=%wide.region_2.3_spmd.clone.clone, body=%wide.region_0.2_spmd.clone.clone.sunk | while | flops 550182976 | bytes 17088796 | solution.py:127
  26.3 1.2 fusion.172
  27.5 4.9 %fusion.173 = f32[16,256,128]{2,1,0:T(8,128)} fusion(bf16[16,128,512]{2,1,0:T(8,128)(2,1)S(1)} %get-tuple-element.251, bf16[16,128,512]{2,1,0:T(8,128)(2,1)S(1)} %get-tuple-element.252, s32[16,512]{1,0:T(8,128)S(1)} %get-tuple-element.253), kind=kOutput, calls=%fused_computation.2.clone.1 | convolution fusion | flops 546308096 | bytes 6324224 | tf_op jit(solution)/shard_map/while/body/eval_jaxpr/gab,gbc->gac/dot_general | solution.py:119
  32.5 0.7 fusion.171
  33.2 3.7 %scatter_fusion = f32[2,128,16,128]{3,1,2,0:T(8,128)S(1)} fusion(f32[2,128,16,128]{3,1,2,0:T(8,128)S(1)} %get-tuple-element.262, s32[16]{0:T(128)S(1)} %fusion.171, f32[16,2,128,128]{3,2,1,0:T(8,128)} %bitcast.135), kind=kCustom, calls=%fused_computation.clone.clone.1 | custom fusion | flops 524288 | bytes 6291520 | tf_op jit(solution)/shard_map/while/body/eval_jaxpr/scatter-add | solution.py:123
  36.9 1.2 fusion.172
  38.1 4.9 %fusion.173 = f32[16,256,128]{2,1,0:T(8,128)} fusion(bf16[16,128,512]{2,1,0:T(8,128)(2,1)S(1)} %get-tuple-element.251, bf16[16,128,512]{2,1,0:T(8,128)(2,1)S(1)} %get-tuple-element.252, s32[16,512]{1,0:T(8,128)S(1)} %get-tuple-element.253), kind=kOutput, calls=%fused_computation.2.clone.1 | convolution fusion | flops 546308096 | bytes 6324224 | tf_op jit(solution)/shard_map/while/body/eval_jaxpr/gab,gbc->gac/dot_general | solution.py:119
  43.1 0.7 fusion.171
  43.8 3.7 %scatter_fusion = f32[2,128,16,128]{3,1,2,0:T(8,128)S(1)} fusion(f32[2,128,16,128]{3,1,2,0:T(8,128)S(1)} %get-tuple-element.262, s32[16]{0:T(128)S(1)} %fusion.171, f32[16,2,128,128]{3,2,1,0:T(8,128)} %bitcast.135), kind=kCustom, calls=%fused_computation.clone.clone.1 | custom fusion | flops 524288 | bytes 6291520 | tf_op jit(solution)/shard_map/while/body/eval_jaxpr/scatter-add | solution.py:123
  47.5 1.2 fusion.172
  48.8 4.9 %fusion.173 = f32[16,256,128]{2,1,0:T(8,128)} fusion(bf16[16,128,512]{2,1,0:T(8,128)(2,1)S(1)} %get-tuple-element.251, bf16[16,128,512]{2,1,0:T(8,128)(2,1)S(1)} %get-tuple-element.252, s32[16,512]{1,0:T(8,128)S(1)} %get-tuple-element.253), kind=kOutput, calls=%fused_computation.2.clone.1 | convolution fusion | flops 546308096 | bytes 6324224 | tf_op jit(solution)/shard_map/while/body/eval_jaxpr/gab,gbc->gac/dot_general | solution.py:119
  53.7 0.7 fusion.171
  54.4 3.7 %scatter_fusion = f32[2,128,16,128]{3,1,2,0:T(8,128)S(1)} fusion(f32[2,128,16,128]{3,1,2,0:T(8,128)S(1)} %get-tuple-element.262, s32[16]{0:T(128)S(1)} %fusion.171, f32[16,2,128,128]{3,2,1,0:T(8,128)} %bitcast.135), kind=kCustom, calls=%fused_computation.clone.clone.1 | custom fusion | flops 524288 | bytes 6291520 | tf_op jit(solution)/shard_map/while/body/eval_jaxpr/scatter-add | solution.py:123
  58.2 1.2 fusion.172
  59.4 4.9 %fusion.173 = f32[16,256,128]{2,1,0:T(8,128)} fusion(bf16[16,128,512]{2,1,0:T(8,128)(2,1)S(1)} %get-tuple-element.251, bf16[16,128,512]{2,1,0:T(8,128)(2,1)S(1)} %get-tuple-element.252, s32[16,512]{1,0:T(8,128)S(1)} %get-tuple-element.253), kind=kOutput, calls=%fused_computation.2.clone.1 | convolution fusion | flops 546308096 | bytes 6324224 | tf_op jit(solution)/shard_map/while/body/eval_jaxpr/gab,gbc->gac/dot_general | solution.py:119
  64.4 0.7 fusion.171
  65.1 3.6 %scatter_fusion = f32[2,128,16,128]{3,1,2,0:T(8,128)S(1)} fusion(f32[2,128,16,128]{3,1,2,0:T(8,128)S(1)} %get-tuple-element.262, s32[16]{0:T(128)S(1)} %fusion.171, f32[16,2,128,128]{3,2,1,0:T(8,128)} %bitcast.135), kind=kCustom, calls=%fused_computation.clone.clone.1 | custom fusion | flops 524288 | bytes 6291520 | tf_op jit(solution)/shard_map/while/body/eval_jaxpr/scatter-add | solution.py:123
  68.8 1.2 fusion.172
  70.0 4.9 %fusion.173 = f32[16,256,128]{2,1,0:T(8,128)} fusion(bf16[16,128,512]{2,1,0:T(8,128)(2,1)S(1)} %get-tuple-element.251, bf16[16,128,512]{2,1,0:T(8,128)(2,1)S(1)} %get-tuple-element.252, s32[16,512]{1,0:T(8,128)S(1)} %get-tuple-element.253), kind=kOutput, calls=%fused_computation.2.clone.1 | convolution fusion | flops 546308096 | bytes 6324224 | tf_op jit(solution)/shard_map/while/body/eval_jaxpr/gab,gbc->gac/dot_general | solution.py:119
  75.0 0.7 fusion.171
  75.7 3.7 %scatter_fusion = f32[2,128,16,128]{3,1,2,0:T(8,128)S(1)} fusion(f32[2,128,16,128]{3,1,2,0:T(8,128)S(1)} %get-tuple-element.262, s32[16]{0:T(128)S(1)} %fusion.171, f32[16,2,128,128]{3,2,1,0:T(8,128)} %bitcast.135), kind=kCustom, calls=%fused_computation.clone.clone.1 | custom fusion | flops 524288 | bytes 6291520 | tf_op jit(solution)/shard_map/while/body/eval_jaxpr/scatter-add | solution.py:123
  79.4 1.2 fusion.172
  80.7 4.9 %fusion.173 = f32[16,256,128]{2,1,0:T(8,128)} fusion(bf16[16,128,512]{2,1,0:T(8,128)(2,1)S(1)} %get-tuple-element.251, bf16[16,128,512]{2,1,0:T(8,128)(2,1)S(1)} %get-tuple-element.252, s32[16,512]{1,0:T(8,128)S(1)} %get-tuple-element.253), kind=kOutput, calls=%fused_computation.2.clone.1 | convolution fusion | flops 546308096 | bytes 6324224 | tf_op jit(solution)/shard_map/while/body/eval_jaxpr/gab,gbc->gac/dot_general | solution.py:119
  85.6 0.7 fusion.171
  86.3 3.7 %scatter_fusion = f32[2,128,16,128]{3,1,2,0:T(8,128)S(1)} fusion(f32[2,128,16,128]{3,1,2,0:T(8,128)S(1)} %get-tuple-element.262, s32[16]{0:T(128)S(1)} %fusion.171, f32[16,2,128,128]{3,2,1,0:T(8,128)} %bitcast.135), kind=kCustom, calls=%fused_computation.clone.clone.1 | custom fusion | flops 524288 | bytes 6291520 | tf_op jit(solution)/shard_map/while/body/eval_jaxpr/scatter-add | solution.py:123
  90.1 1.2 fusion.172
  91.3 4.9 %fusion.173 = f32[16,256,128]{2,1,0:T(8,128)} fusion(bf16[16,128,512]{2,1,0:T(8,128)(2,1)S(1)} %get-tuple-element.251, bf16[16,128,512]{2,1,0:T(8,128)(2,1)S(1)} %get-tuple-element.252, s32[16,512]{1,0:T(8,128)S(1)} %get-tuple-element.253), kind=kOutput, calls=%fused_computation.2.clone.1 | convolution fusion | flops 546308096 | bytes 6324224 | tf_op jit(solution)/shard_map/while/body/eval_jaxpr/gab,gbc->gac/dot_general | solution.py:119
  96.2 0.7 fusion.171
  96.9 3.7 %scatter_fusion = f32[2,128,16,128]{3,1,2,0:T(8,128)S(1)} fusion(f32[2,128,16,128]{3,1,2,0:T(8,128)S(1)} %get-tuple-element.262, s32[16]{0:T(128)S(1)} %fusion.171, f32[16,2,128,128]{3,2,1,0:T(8,128)} %bitcast.135), kind=kCustom, calls=%fused_computation.clone.clone.1 | custom fusion | flops 524288 | bytes 6291520 | tf_op jit(solution)/shard_map/while/body/eval_jaxpr/scatter-add | solution.py:123
  100.7 1.2 fusion.172
  101.9 4.9 %fusion.173 = f32[16,256,128]{2,1,0:T(8,128)} fusion(bf16[16,128,512]{2,1,0:T(8,128)(2,1)S(1)} %get-tuple-element.251, bf16[16,128,512]{2,1,0:T(8,128)(2,1)S(1)} %get-tuple-element.252, s32[16,512]{1,0:T(8,128)S(1)} %get-tuple-element.253), kind=kOutput, calls=%fused_computation.2.clone.1 | convolution fusion | flops 546308096 | bytes 6324224 | tf_op jit(solution)/shard_map/while/body/eval_jaxpr/gab,gbc->gac/dot_general | solution.py:119
  106.9 0.7 fusion.171
  107.6 3.6 %scatter_fusion = f32[2,128,16,128]{3,1,2,0:T(8,128)S(1)} fusion(f32[2,128,16,128]{3,1,2,0:T(8,128)S(1)} %get-tuple-element.262, s32[16]{0:T(128)S(1)} %fusion.171, f32[16,2,128,128]{3,2,1,0:T(8,128)} %bitcast.135), kind=kCustom, calls=%fused_computation.clone.clone.1 | custom fusion | flops 524288 | bytes 6291520 | tf_op jit(solution)/shard_map/while/body/eval_jaxpr/scatter-add | solution.py:123
  111.2 1.8 copy.63
  113.0 4.2 %copy.64 = f32[2,128,2048]{2,0,1:T(2,128)} copy(f32[2,128,2048]{1,2,0:T(8,128)} %bitcast.136) | data formatting | bytes 4194304 | tf_op jit(solution)/shard_map/reshape | solution.py:128
  117.3 0.6 copy-done.1
  117.9 0.6 dynamic-slice
  119.2 86.3 %all-reduce.3.cloned.1.call-done = f32[2,128,2048]{2,0,1:T(2,128)} async-done(((f32[2,128,2048]{2,0,1:T(2,128)}), f32[2,128,2048]{2,0,1:T(2,128)}) %all-reduce.3.cloned.1.call-update) | async-done | bytes 2097168
  205.5 1.1 constant_dynamic-slice_fusion.1
  206.6 18.4 %fusion.33 = f32[2,1,512,32]{2,3,0,1:T(8,128)S(1)} fusion(f32[2,32,2048]{2,0,1:T(2,128)S(1)} %constant_dynamic-slice_fusion.1), kind=kOutput, calls=%fused_computation.51 | convolution fusion | flops 819986432 | bytes 655360 | tf_op jit(solution)/shard_map/cry,yk->ckr/dot_general | solution.py:34
  225.0 18.6 %fusion.39 = f32[2,1,512,32]{2,3,0,1:T(8,128)S(1)} fusion(f32[2,32,2048]{2,0,1:T(2,128)S(1)} %constant_dynamic-slice_fusion.1), kind=kOutput, calls=%fused_computation.53 | convolution fusion | flops 820019200 | bytes 655360 | tf_op jit(solution)/shard_map/cry,yk->ckr/dot_general | solution.py:35
  243.6 0.7 copy.67
  244.3 1.8 reshape.526
  246.1 3.7 %all-to-all-start = ((f32[4,1,16384]{2,1,0:T(1,128)}), f32[4,1,16384]{2,1,0:T(1,128)S(1)}, u32[]{:S(2)}, u32[]{:S(2)}) async-start(f32[4,1,16384]{2,1,0:T(1,128)} %reshape.526), calls=%async_computation | async-start | bytes 524288 | tf_op jit(solution)/shard_map/all_to_all | solution.py:132
  249.8 8.8 %all-to-all-done = f32[4,1,16384]{2,1,0:T(1,128)S(1)} async-done(((f32[4,1,16384]{2,1,0:T(1,128)}), f32[4,1,16384]{2,1,0:T(1,128)S(1)}, u32[]{:S(2)}, u32[]{:S(2)}) %all-to-all-start) | async-done | bytes 262176 | tf_op jit(solution)/shard_map/all_to_all | solution.py:132
  259.2 1.4 reduce.66
  260.6 0.9 reshape.527
  261.5 0.8 copy.87
  262.3 0.8 copy.70
  263.1 3.4 %all-to-all-start.1 = ((f32[2,2,128,128]{3,1,0,2:T(2,128)}), f32[2,2,128,128]{3,1,0,2:T(2,128)S(1)}, u32[]{:S(2)}, u32[]{:S(2)}) async-start(f32[2,2,128,128]{3,1,0,2:T(2,128)} %copy.70), calls=%async_computation.1 | async-start | bytes 524288 | tf_op jit(solution)/shard_map/all_to_all | solution.py:131
  266.6 6.0 %all-to-all-done.1 = f32[2,2,128,128]{3,1,0,2:T(2,128)S(1)} async-done(((f32[2,2,128,128]{3,1,0,2:T(2,128)}), f32[2,2,128,128]{3,1,0,2:T(2,128)S(1)}, u32[]{:S(2)}, u32[]{:S(2)}) %all-to-all-start.1) | async-done | bytes 262176 | tf_op jit(solution)/shard_map/all_to_all | solution.py:131
  273.0 0.5 fusion.74
  277.6 0.7 pad_maximum_fusion.3
  278.2 0.7 pad_maximum_fusion.2
  (64 shorter events, 6.8 us)
Async XLA Ops:
  7.2 7.0 %copy-start = (f32[7,33]{1,0:T(8,128)S(1)}, f32[7,33]{1,0:T(8,128)}, u32[]{:S(2)}) copy-start(f32[7,33]{1,0:T(8,128)} %param.16) | copy-start | bytes 2776
  7.2 198.3 %all-reduce.3.cloned.1.call-start = ((), (), s32[]{:S(2)}) async-start(), calls=%async_computation.2 | async-start | bytes 4194304
  8.0 11.3 %collective-permute-start.1 = (bf16[8,16]{1,0:T(8,128)(2,1)S(1)}, bf16[8,16]{1,0:T(8,128)(2,1)S(1)}, u32[]{:S(2)}, u32[]{:S(2)}) collective-permute-start(bf16[8,16]{1,0:T(8,128)(2,1)S(1)} %get-tuple-element.196), channel_id=1, source_target_pairs={{2,0},{3,1},{6,4},{7,5},{10,8},{11,9},{14,12},{15,13},{18,16},{19,... | collective-permute-start | bytes 776 | tf_op jit(solution)/shard_map/ppermute | solution.py:25
  9.3 10.1 %collective-permute-start = (bf16[8,16]{1,0:T(8,128)(2,1)S(1)}, bf16[8,16]{1,0:T(8,128)(2,1)S(1)}, u32[]{:S(2)}, u32[]{:S(2)}) collective-permute-start(bf16[8,16]{1,0:T(8,128)(2,1)S(1)} %get-tuple-element.195), channel_id=1, source_target_pairs={{0,2},{1,3},{4,6},{5,7},{8,10},{9,11},{12,14},{13,15},{16,18},{17,... | collective-permute-start | bytes 776 | tf_op jit(solution)/shard_map/ppermute | solution.py:22
  117.3 0.7 copy-start.1
  246.1 12.6 %all-to-all-start = ((f32[4,1,16384]{2,1,0:T(1,128)}), f32[4,1,16384]{2,1,0:T(1,128)S(1)}, u32[]{:S(2)}, u32[]{:S(2)}) async-start(f32[4,1,16384]{2,1,0:T(1,128)} %reshape.526), calls=%async_computation | async-start | bytes 524288 | tf_op jit(solution)/shard_map/all_to_all | solution.py:132
  263.1 9.4 %all-to-all-start.1 = ((f32[2,2,128,128]{3,1,0,2:T(2,128)}), f32[2,2,128,128]{3,1,0,2:T(2,128)S(1)}, u32[]{:S(2)}, u32[]{:S(2)}) async-start(f32[2,2,128,128]{3,1,0,2:T(2,128)} %copy.70), calls=%async_computation.1 | async-start | bytes 524288 | tf_op jit(solution)/shard_map/all_to_all | solution.py:131
Sparse Core Ops, SparseCore 0:
  117.4 88.0 all-reduce.2
where the time goes:
time: 287 us; the launch traced here: 286 us
  waiting for transfers between devices  101 us (35%)
  matrix products  81.1 us (28%)
  other arithmetic  55.9 us (19%)
  local copies, waits for them, and re-layouts  18.9 us (7%)
  between operations  15 us (5%)
  starting transfers between devices  13.2 us (5%)
    unnamed x2, waiting for transfers between devices  86.3 us
    dot_general x8, matrix products, bin_step(): jnp.einsum('gab,gbc->gac', weighted, col_hot, preferred_element_type=jnp....  39.5 us
    scatter-add x8, other arithmetic, bin_step(): band_map = band_map.at[:, :, tile_part, :].add(tile_sums)  29.2 us
    dot_general x1, matrix products, transform_rows(): jnp.einsum('cry,yk->ckr', strip_map, jnp.sin(angles), precision=HIGH)  18.6 us
    dot_general x1, matrix products, transform_rows(): jnp.einsum('cry,yk->ckr', strip_map, jnp.cos(angles), precision=HIGH)  18.4 us
    select_n x8, other arithmetic, bin_step(): jnp.where(row_hot, q_part[:, None, :], zero_value)  9.8 us
    all_to_all x1, waiting for transfers between devices, body(): lax.all_to_all(spectrum, 'det', split_axis=2, concat_axis=3, tiled=True)  8.83 us
    unnamed x10, local copies, waits for them, and re-layouts  7.01 us
  transfers between devices with their start and end apart: 5, of which 3 were waited for; matrix products, arithmetic and copies ran while one was open for 2% of the time, Pallas kernels for 0%

commit v1 on v0

v1 whole, which is shorter than its diff:
```python
import math

import jax
import jax.numpy as jnp
import ml_dtypes
import numpy as np
from jax import lax
from jax.experimental import pallas as pl
from jax.experimental.pallas import tpu as pltpu
from jax.sharding import PartitionSpec as P

TILE = 128
MAPY = 2048
KY = 512
NANG = 8192
LANES = 128
CHUNK = 1024
HIGH = lax.Precision.HIGHEST
MESH = pl.DeviceIdType.MESH
NT = (((1,), (1,)), ((), ()))


def split_np(table):
    table = table.astype(np.float32)
    high = table.astype(ml_dtypes.bfloat16)
    low = (table - high.astype(np.float32)).astype(ml_dtypes.bfloat16)
    return high, low


def split(value):
    high = value.astype(jnp.bfloat16)
    return high, (value - high.astype(jnp.float32)).astype(jnp.bfloat16)


def row_tables(owners):
    kept = KY // owners
    ky = np.arange(KY).reshape(owners, 1, kept // 2, 2)
    ky = np.moveaxis(ky, 3, 0)
    y = np.arange(MAPY // 2)
    angle = (ky[..., None] * y % MAPY) * (2.0 * np.pi / MAPY)
    table = np.concatenate([np.cos(angle), -np.sin(angle)], axis=2)
    return split_np(table.reshape(2, KY, MAPY // 2))


def column_tables(length):
    pos = np.arange(length)
    angle = (pos[:, None] * pos[None, :] % length) * (2.0 * np.pi / length)
    table = np.concatenate([np.cos(angle), np.sin(angle)], axis=1)
    return split_np(table / math.sqrt(length * MAPY))


def halos(block, width):
    count = lax.axis_size("tm")
    forward = [(i, i + 1) for i in range(count - 1)]
    backward = [(target, source) for source, target in forward]
    low = lax.ppermute(block[:, block.shape[1] - width :], "tm", forward)
    high = lax.ppermute(block[:, :width], "tm", backward)
    return low, high


def bin_kernel(
    tile_ref, ts_ref, low_ref, high_ref, hwp_ref, flags_ref, pix_ref, wafer_ref, taps_ref,
    angle_ref, thigh_ref, tlow_ref, out_ref,
    xs, cos_h, sin_h, q_s, u_s, map_s,
):
    det_rows, time_len = ts_ref.shape
    tap_count = taps_ref.shape[1]
    width = (tap_count - 1) // 2
    block_count = tile_ref.shape[1]
    block_len = time_len // block_count

    xs[:, 0:LANES] = jnp.zeros((det_rows, LANES), jnp.float32)
    xs[:, LANES + time_len :] = jnp.zeros((det_rows, LANES), jnp.float32)
    xs[:, LANES : LANES + time_len] = ts_ref[...].astype(jnp.float32)
    xs[:, LANES - width : LANES] = low_ref[...].astype(jnp.float32)
    xs[:, LANES + time_len : LANES + time_len + width] = high_ref[...].astype(jnp.float32)
    wafer = wafer_ref[...]
    det_taps = jnp.zeros((det_rows, tap_count), jnp.float32)
    for w in range(taps_ref.shape[0]):
        det_taps = det_taps + jnp.where(wafer == w, taps_ref[w : w + 1, :], 0.0)
    hwp = (4 * hwp_ref[...] % NANG).astype(jnp.float32) * (2.0 * math.pi / NANG)
    cos_h[...] = jnp.cos(hwp)
    sin_h[...] = jnp.sin(hwp)
    twice = 2.0 * angle_ref[...]
    cos_a = jnp.cos(twice)
    sin_a = jnp.sin(twice)
    chunk = min(CHUNK, time_len)
    span = chunk + 2 * LANES
    per = chunk // LANES

    @pl.loop(0, time_len // chunk)
    def _(step):
        start = pl.multiple_of(step * chunk, chunk)
        base = xs[:, pl.ds(start, span)]
        total = jnp.zeros((det_rows, chunk), jnp.float32)
        for j in range(tap_count):
            moved = pltpu.roll(base, span - (LANES - width + j), 1)
            total = total + det_taps[:, j : j + 1] * moved[:, :chunk]
        flagged = total * flags_ref[:, pl.ds(start, chunk)].astype(jnp.float32)
        rows = pl.ds(pl.multiple_of(step * per, per), per)
        ch = cos_h[rows, :]
        sh = sin_h[rows, :]
        for k in range(per):
            lanes = pl.ds(pl.multiple_of(start + k * LANES, LANES), LANES)
            part = flagged[:, k * LANES : (k + 1) * LANES]
            c = ch[k : k + 1, :]
            s = sh[k : k + 1, :]
            q_s[:, lanes] = part * (c * cos_a + s * sin_a)
            u_s[:, lanes] = part * (s * cos_a - c * sin_a)

    map_s[...] = jnp.zeros(map_s.shape, jnp.float32)
    sub = 16
    side = lax.broadcasted_iota(jnp.int32, (sub, block_len), 0).astype(jnp.float32)
    zero = jnp.zeros((sub, block_len), jnp.bfloat16)
    one = jnp.ones((sub, block_len), jnp.bfloat16)
    ids = [(side + float(g * sub)).astype(jnp.bfloat16) for g in range(TILE // sub)]

    def spread(row):
        return jnp.broadcast_to(row, (sub, block_len)).astype(jnp.bfloat16)

    @pl.loop(0, block_count)
    def _(b):
        lanes = pl.ds(pl.multiple_of(b * block_len, block_len), block_len)
        for d in range(det_rows):
            pix = pix_ref[d : d + 1, lanes]
            row_id = spread((pix // TILE).astype(jnp.float32))
            col_id = spread((pix % TILE).astype(jnp.float32))
            qv = spread(q_s[d : d + 1, lanes])
            uv = spread(u_s[d : d + 1, lanes])
            hits = [row_id == i for i in ids]
            weighted = jnp.concatenate(
                [jnp.where(h, qv, zero) for h in hits] + [jnp.where(h, uv, zero) for h in hits],
                axis=0,
            )
            col_hot = jnp.concatenate([jnp.where(col_id == i, one, zero) for i in ids], axis=0)
            sums = lax.dot_general(weighted, col_hot, NT, preferred_element_type=jnp.float32)
            tile = tile_ref[d, b]
            map_s[tile] = map_s[tile] + sums

    tiles = MAPY // TILE
    first = jnp.concatenate([map_s[t] for t in range(tiles // 2)], axis=1)
    second = jnp.concatenate([map_s[t] for t in range(tiles // 2, tiles)], axis=1)
    for parity in range(2):
        folded = first + second if parity == 0 else first - second
        f_high, f_low = split(folded)
        t_high = thigh_ref[parity]
        acc = lax.dot_general(t_high, f_high, NT, preferred_element_type=jnp.float32)
        acc = acc + lax.dot_general(t_high, f_low, NT, preferred_element_type=jnp.float32)
        acc = acc + lax.dot_general(
            tlow_ref[parity], f_high, NT, preferred_element_type=jnp.float32
        )
        out_ref[2 * parity] = acc[:, :TILE].astype(jnp.bfloat16)
        out_ref[2 * parity + 1] = acc[:, TILE:].astype(jnp.bfloat16)


def local_spectrum(timestream, hwp_index, flags, pixel_index, tile_index, wafer, taps, angle, owners):
    det_rows, time_len = timestream.shape
    width = (taps.shape[1] - 1) // 2
    low, high = halos(timestream, width)
    t_high, t_low = row_tables(owners)
    vmem = pl.BlockSpec(memory_space=pltpu.VMEM)
    return pl.pallas_call(
        bin_kernel,
        out_shape=jax.ShapeDtypeStruct((4, KY, TILE), jnp.bfloat16),
        in_specs=[pl.BlockSpec(memory_space=pltpu.SMEM)] + [vmem] * 11,
        out_specs=vmem,
        scratch_shapes=[
            pltpu.VMEM((det_rows, time_len + 2 * LANES), jnp.float32),
            pltpu.VMEM((time_len // LANES, LANES), jnp.float32),
            pltpu.VMEM((time_len // LANES, LANES), jnp.float32),
            pltpu.VMEM((det_rows, time_len), jnp.float32),
            pltpu.VMEM((det_rows, time_len), jnp.float32),
            pltpu.VMEM((MAPY // TILE, 2 * TILE, TILE), jnp.float32),
        ],
        compiler_params=pltpu.CompilerParams(vmem_limit_bytes=40 * 2**20),
        name="bin_and_rows",
    )(
        tile_index, timestream, low, high, hwp_index.reshape(time_len // LANES, LANES), flags,
        pixel_index, wafer[:, None], taps, angle[:, None], jnp.asarray(t_high), jnp.asarray(t_low),
    )


def rotation(kx, length, ky):
    fx = jnp.where(kx < length // 2, kx, kx - length).astype(jnp.float32)
    fy = ky.astype(jnp.float32)
    radius = jnp.maximum(fx * fx + fy * fy, 1.0)
    return (fx * fx - fy * fy) / radius, 2.0 * fx * fy / radius


def exchange_kernel(sizes, spec_ref, whigh_ref, wlow_ref, e_ref, b_ref, recv, ordered, send_sem, recv_sem):
    n_det, n_tm, n_pol = sizes
    owners = n_det * n_tm * n_pol
    strips = n_tm * n_pol
    kept = KY // owners
    half = kept // 2
    length = strips * TILE
    me = (lax.axis_index("det") * n_tm + lax.axis_index("tm")) * n_pol + lax.axis_index("pol")

    def place(index):
        return {
            "det": index // strips,
            "tm": lax.rem(index // n_pol, n_tm),
            "pol": lax.rem(index, n_pol),
        }

    barrier = pltpu.get_barrier_semaphore()
    for step in range(1, owners):
        peer = lax.rem(me + step, owners)
        pl.semaphore_signal(barrier, inc=1, device_id=place(peer), device_id_type=MESH)
    pl.semaphore_wait(barrier, owners - 1)

    copies = []
    for step in range(1, owners):
        peer = lax.rem(me + step, owners)
        copy = pltpu.make_async_remote_copy(
            src_ref=spec_ref.at[:, pl.ds(pl.multiple_of(peer * kept, kept), kept), :],
            dst_ref=recv.at[me],
            send_sem=send_sem.at[step],
            recv_sem=recv_sem.at[step],
            device_id=place(peer),
            device_id_type=MESH,
        )
        copy.start()
        copies.append(copy)
    recv[me] = spec_ref[:, pl.ds(pl.multiple_of(me * kept, kept), kept), :]
    kx = lax.broadcasted_iota(jnp.int32, (kept, length), 1)
    ky = me * kept + lax.broadcasted_iota(jnp.int32, (kept, length), 0)
    cosine, sine = rotation(kx, length, ky)
    for copy in copies:
        copy.wait()

    columns = []
    for strip in range(strips):
        total = recv[strip].astype(jnp.float32)
        for det in range(1, n_det):
            total = total + recv[det * strips + strip].astype(jnp.float32)
        for parity in range(2):
            for c in range(2):
                for part in range(2):
                    ordered[strip, c, part, pl.ds(parity, half, stride=2), :] = total[
                        2 * parity + c, part * half : (part + 1) * half
                    ]
        columns.append(ordered[strip].reshape(4 * kept, TILE))
    x_high, x_low = split(jnp.concatenate(columns, axis=1))
    w_high = whigh_ref[...]
    acc = jnp.dot(x_high, w_high, preferred_element_type=jnp.float32)
    acc = acc + jnp.dot(x_low, w_high, preferred_element_type=jnp.float32)
    acc = acc + jnp.dot(x_high, wlow_ref[...], preferred_element_type=jnp.float32)
    real, imag = [], []
    for c in range(2):
        re_rows = slice(2 * c * kept, (2 * c + 1) * kept)
        im_rows = slice((2 * c + 1) * kept, (2 * c + 2) * kept)
        real.append(acc[re_rows, :length] + acc[im_rows, length:])
        imag.append(acc[im_rows, :length] - acc[re_rows, length:])
    e_ref[0] = cosine * real[0] + sine * real[1]
    e_ref[1] = cosine * imag[0] + sine * imag[1]
    b_ref[0] = cosine * real[1] - sine * real[0]
    b_ref[1] = cosine * imag[1] - sine * imag[0]


def exchange(spec, sizes):
    owners = math.prod(sizes)
    kept = KY // owners
    length = sizes[1] * sizes[2] * TILE
    w_high, w_low = column_tables(length)
    vmem = pl.BlockSpec(memory_space=pltpu.VMEM)
    shape = jax.ShapeDtypeStruct((2, kept, length), jnp.float32)

    def kernel(*refs):
        exchange_kernel(sizes, *refs)

    return pl.pallas_call(
        kernel,
        out_shape=(shape, shape),
        in_specs=[vmem] * 3,
        out_specs=(vmem, vmem),
        scratch_shapes=[
            pltpu.VMEM((owners, 4, kept, TILE), jnp.bfloat16),
            pltpu.VMEM((sizes[1] * sizes[2], 2, 2, kept, TILE), jnp.float32),
            pltpu.SemaphoreType.DMA((owners,)),
            pltpu.SemaphoreType.DMA((owners,)),
        ],
        compiler_params=pltpu.CompilerParams(
            collective_id=0, has_side_effects=True, vmem_limit_bytes=40 * 2**20
        ),
        name="exchange_and_columns",
    )(spec, jnp.asarray(w_high), jnp.asarray(w_low))


def twiddle_table(first, second, length):
    return (first * second % length).astype(jnp.float32) * (2.0 * math.pi / length)


def transform_columns(real_in, imag_in):
    lead, kept, length = real_in.shape
    outer = TILE
    inner = length // outer
    real_grid = real_in.reshape(lead, kept, outer, inner)
    imag_grid = imag_in.reshape(lead, kept, outer, inner)
    outer_pos = jnp.arange(outer, dtype=jnp.int32)
    inner_pos = jnp.arange(inner, dtype=jnp.int32)
    first_angle = twiddle_table(outer_pos[:, None], outer_pos[None, :], outer)
    first_cos = jnp.cos(first_angle)
    first_sin = jnp.sin(first_angle)
    section_real = jnp.einsum("ckab,ad->ckdb", real_grid, first_cos, precision=HIGH) + jnp.einsum(
        "ckab,ad->ckdb", imag_grid, first_sin, precision=HIGH
    )
    section_imag = jnp.einsum("ckab,ad->ckdb", imag_grid, first_cos, precision=HIGH) - jnp.einsum(
        "ckab,ad->ckdb", real_grid, first_sin, precision=HIGH
    )
    mid_angle = twiddle_table(outer_pos[:, None], inner_pos[None, :], length)
    mid_cos = jnp.cos(mid_angle)
    mid_sin = jnp.sin(mid_angle)
    turned_real = section_real * mid_cos + section_imag * mid_sin
    turned_imag = section_imag * mid_cos - section_real * mid_sin
    last_angle = twiddle_table(inner_pos[:, None], inner_pos[None, :], inner)
    last_cos = jnp.cos(last_angle)
    last_sin = jnp.sin(last_angle)
    final_real = jnp.einsum("ckdb,be->cked", turned_real, last_cos, precision=HIGH) + jnp.einsum(
        "ckdb,be->cked", turned_imag, last_sin, precision=HIGH
    )
    final_imag = jnp.einsum("ckdb,be->cked", turned_imag, last_cos, precision=HIGH) - jnp.einsum(
        "ckdb,be->cked", turned_real, last_sin, precision=HIGH
    )
    return (final_real.reshape(lead, kept, length), final_imag.reshape(lead, kept, length))


def exchange_many(spec, sizes):
    n_det, n_tm, n_pol = sizes
    owners = math.prod(sizes)
    kept = KY // owners
    half = kept // 2
    strips = n_tm * n_pol
    length = strips * TILE
    pieces = spec.reshape(2, 2, owners, 2, half, TILE)
    moved = lax.all_to_all(pieces, ("det", "tm", "pol"), split_axis=2, concat_axis=2, tiled=True)
    summed = jnp.sum(moved.reshape(2, 2, n_det, strips, 2, half, TILE).astype(jnp.float32), axis=2)
    columns = jnp.transpose(summed, (3, 1, 4, 0, 2, 5)).reshape(2, 2, kept, length)
    final_real, final_imag = transform_columns(columns[0], columns[1])
    norm_scale = 1.0 / math.sqrt(length * MAPY)
    real = final_real * norm_scale
    imag = final_imag * norm_scale
    position = (lax.axis_index("det") * n_tm + lax.axis_index("tm")) * n_pol + lax.axis_index("pol")
    cosine, sine = rotation(
        jnp.arange(length, dtype=jnp.int32)[None, :],
        length,
        (position * kept + jnp.arange(kept, dtype=jnp.int32))[:, None],
    )
    return (
        jnp.stack([cosine * real[0] + sine * real[1], cosine * imag[0] + sine * imag[1]]),
        jnp.stack([cosine * real[1] - sine * real[0], cosine * imag[1] - sine * imag[0]]),
    )


def solution(mesh):
    sizes = (mesh.shape["det"], mesh.shape["tm"], mesh.shape["pol"])
    owners = math.prod(sizes)

    def body(*args):
        spec = local_spectrum(*args, owners)
        if KY // owners % 16 == 0:
            return exchange(spec, sizes)
        return exchange_many(spec, sizes)

    in_specs = (
        P(("group", "det", "pol"), "tm"),
        P(("group", "tm")),
        P(("group", "det", "pol"), "tm"),
        P(("group", "det", "pol"), "tm"),
        P(("group", "det", "pol"), "tm"),
        P(("group", "det", "pol")),
        P(),
        P(("group", "det", "pol")),
    )
    out_specs = (
        P(None, ("group", "det", "tm", "pol"), None),
        P(None, ("group", "det", "tm", "pol"), None),
    )
    return jax.shard_map(body, mesh=mesh, in_specs=in_specs, out_specs=out_specs, check_vma=False)
```

time: 287 us -> 54.9 us (0.19)
  the two profiles are of different devices: /device:TPU:0 before, /device:TPU:11 now
where the time goes in v1:
time: 54.9 us; the launch traced here: 54.4 us
  Pallas kernels  37 us (67%)
  local copies, waits for them, and re-layouts  11.7 us (21%)
  starting transfers between devices  3.44 us (6%)
  waiting for transfers between devices  1.57 us (3%)
  between operations  0.69 us (1%)
    pallas_call x1, Pallas kernels, exchange(): pl.pallas_call(kernel, out_shape=(shape, shape), in_specs=[vmem] * 3, out...  19 us
    pallas_call x1, Pallas kernels, local_spectrum(): pl.pallas_call(bin_kernel, out_shape=jax.ShapeDtypeStruct((4, KY, TILE),...  18 us
    unnamed x22, local copies, waits for them, and re-layouts  9.43 us
    ppermute x1, starting transfers between devices, halos(): high = lax.ppermute(block[:, :width], 'tm', backward)  2.15 us
    ppermute x1, waiting for transfers between devices, halos(): low = lax.ppermute(block[:, block.shape[1] - width:], 'tm', forward)  1.56 us
    ppermute x1, starting transfers between devices, halos(): low = lax.ppermute(block[:, block.shape[1] - width:], 'tm', forward)  1.29 us
  transfers between devices with their start and end apart: 2, of which 1 were waited for; matrix products, arithmetic and copies ran while one was open for 3% of the time, Pallas kernels for 0%

profile of v1, /device:TPU:11, one launch (start us, length us, event | category | flops | bytes accessed | tf_op | source)
XLA Modules:
  0.0 54.4 jit_solution(8288463419482879560)
XLA Ops:
  0.6 0.8 %fusion = (bf16[8,16]{1,0:T(8,128)(2,1)S(1)}, bf16[8,16]{1,0:T(8,128)(2,1)S(1)}) fusion(bf16[8,8192]{1,0:T(8,128)(2,1)} %ts_ref.1), kind=kLoop, calls=%fused_computation | loop fusion | bytes 1024 | tf_op jit(solution)/shard_map/slice | solution.py:57
  1.4 2.1 %collective-permute-start.1 = (bf16[8,16]{1,0:T(8,128)(2,1)S(1)}, bf16[8,16]{1,0:T(8,128)(2,1)S(1)}, u32[]{:S(2)}, u32[]{:S(2)}) collective-permute-start(bf16[8,16]{1,0:T(8,128)(2,1)S(1)} %get-tuple-element.2), channel_id=1, source_target_pairs={{2,0},{3,1},{6,4},{7,5},{10,8},{11,9},{14,12},{15,13},{18,16},{19,... | collective-permute-start | bytes 776 | tf_op jit(solution)/shard_map/ppermute | solution.py:57
  3.6 1.3 %collective-permute-start = (bf16[8,16]{1,0:T(8,128)(2,1)S(1)}, bf16[8,16]{1,0:T(8,128)(2,1)S(1)}, u32[]{:S(2)}, u32[]{:S(2)}) collective-permute-start(bf16[8,16]{1,0:T(8,128)(2,1)S(1)} %get-tuple-element.3), channel_id=1, source_target_pairs={{0,2},{1,3},{4,6},{5,7},{8,10},{9,11},{12,14},{13,15},{16,18},{17,... | collective-permute-start | bytes 776 | tf_op jit(solution)/shard_map/ppermute | solution.py:56
  4.9 0.7 %copy.14.wafer_ref = s32[8,1]{1,0:T(8,128)S(1)} copy(s32[8,1]{0,1:T(1,128)} %bitcast.4) | data formatting | bytes 64 | tf_op jit(solution)/shard_map/broadcast_in_dim | solution.py:179
  5.6 0.7 %copy.15.angle_ref = f32[8,1]{1,0:T(8,128)S(1)} copy(f32[8,1]{0,1:T(1,128)} %bitcast.5) | data formatting | bytes 64 | tf_op jit(solution)/shard_map/broadcast_in_dim | solution.py:179
  6.3 0.0 collective-permute-done.1.high_ref
  6.3 1.6 %collective-permute-done.low_ref = bf16[8,16]{1,0:T(8,128)(2,1)S(1)} collective-permute-done((bf16[8,16]{1,0:T(8,128)(2,1)S(1)}, bf16[8,16]{1,0:T(8,128)(2,1)S(1)}, u32[]{:S(2)}, u32[]{:S(2)}) %collective-permute-start) | collective-permute-done | bytes 288 | tf_op jit(solution)/shard_map/ppermute | solution.py:56
  7.9 0.0 copy-start
  7.9 1.6 %copy-done = bf16[2,512,1024]{2,1,0:T(8,128)(2,1)S(1)} copy-done((bf16[2,512,1024]{2,1,0:T(8,128)(2,1)S(1)}, bf16[2,512,1024]{2,1,0:T(8,128)(2,1)}, u32[]{:S(2)}) %copy-start) | copy-done | bytes 2097176
  9.5 0.0 copy-start.1
  9.5 1.6 %copy-done.1 = bf16[2,512,1024]{2,1,0:T(8,128)(2,1)S(1)} copy-done((bf16[2,512,1024]{2,1,0:T(8,128)(2,1)S(1)}, bf16[2,512,1024]{2,1,0:T(8,128)(2,1)}, u32[]{:S(2)}) %copy-start.1) | copy-done | bytes 2097176
  11.1 0.0 copy-start.4
  11.1 0.9 %copy-done.4 = s32[8,8192]{1,0:T(8,128)S(1)} copy-done((s32[8,8192]{1,0:T(8,128)S(1)}, s32[8,8192]{1,0:T(8,128)}, u32[]{:S(2)}) %copy-start.4) | copy-done | bytes 262168
  12.0 0.0 copy-start.5
  12.0 0.9 %copy-done.5 = s32[8,8192]{1,0:T(8,128)S(1)} copy-done((s32[8,8192]{1,0:T(8,128)S(1)}, s32[8,8192]{1,0:T(8,128)}, u32[]{:S(2)}) %copy-start.5) | copy-done | bytes 262168
  13.0 0.0 copy-start.6
  13.0 0.9 %copy-done.6 = bf16[8,8192]{1,0:T(8,128)(2,1)S(1)} copy-done((bf16[8,8192]{1,0:T(8,128)(2,1)S(1)}, bf16[8,8192]{1,0:T(8,128)(2,1)}, u32[]{:S(2)}) %copy-start.6) | copy-done | bytes 131096
  13.9 0.0 copy-start.7
  13.9 0.8 %copy-done.7 = s32[8192]{0:T(1024)S(1)} copy-done((s32[8192]{0:T(1024)S(1)}, s32[8192]{0:T(1024)}, u32[]{:S(2)}) %copy-start.7) | copy-done | bytes 32792
  14.6 0.0 copy-start.8
  14.6 0.7 %copy-done.8 = s32[8,16]{1,0:T(8,128)S(1)} copy-done((s32[8,16]{1,0:T(8,128)S(1)}, s32[8,16]{1,0:T(8,128)}, u32[]{:S(2)}) %copy-start.8) | copy-done | bytes 536
  15.3 0.0 copy-start.9
  15.3 0.7 %copy-done.9 = f32[7,33]{1,0:T(8,128)S(1)} copy-done((f32[7,33]{1,0:T(8,128)S(1)}, f32[7,33]{1,0:T(8,128)}, u32[]{:S(2)}) %copy-start.9) | copy-done | bytes 948
  16.0 0.0 copy-start.2
  16.0 0.0 copy-start.3
  16.0 18.0 %bin_and_rows.1.refs_0_ = bf16[4,512,128]{2,1,0:T(8,128)(2,1)S(1)} custom-call(s32[8,16]{1,0:T(8,128)S(1)} %copy-done.8, bf16[8,8192]{1,0:T(8,128)(2,1)S(1)} %copy-done.6, bf16[8,16]{1,0:T(8,128)(2,1)S(1)} %collective-permute-done.low_ref, bf16[8,16]{1,0:T(8,128)(2,1)S(1)} %collective-permute-done.1.high_ref, s32[64,128]{1,0:T(8,128)S(1)} %bitcast.3, ...), custom_call_target="tpu_custom_call" | custom-call | tf_op jit(solution)/shard_map/bin_and_rows/pallas_call | solution.py:162
  34.0 0.0 copy-done.2
  34.0 0.0 copy-done.3
  34.0 19.0 %exchange_and_columns.1 = (f32[2,32,512]{2,1,0:T(8,128)S(1)}, f32[2,32,512]{2,1,0:T(8,128)S(1)}) custom-call(bf16[4,512,128]{2,1,0:T(8,128)(2,1)S(1)} %bin_and_rows.1.refs_0_, bf16[512,1024]{1,0:T(8,128)(2,1)S(1)} %copy-done.3, bf16[512,1024]{1,0:T(8,128)(2,1)S(1)} %copy-done.2), custom_call_target="tpu_custom_call" | custom-call | tf_op jit(solution)/shard_map/exchange_and_columns/pallas_call | solution.py:272
  53.1 0.7 %copy.18 = f32[2,32,512]{2,1,0:T(8,128)} copy(f32[2,32,512]{2,1,0:T(8,128)S(1)} %get-tuple-element.6) | data formatting | bytes 262144
  53.7 0.7 %copy.19 = f32[2,32,512]{2,1,0:T(8,128)} copy(f32[2,32,512]{2,1,0:T(8,128)S(1)} %get-tuple-element.7) | data formatting | bytes 262144
Async XLA Ops:
  1.4 4.9 %collective-permute-start.1 = (bf16[8,16]{1,0:T(8,128)(2,1)S(1)}, bf16[8,16]{1,0:T(8,128)(2,1)S(1)}, u32[]{:S(2)}, u32[]{:S(2)}) collective-permute-start(bf16[8,16]{1,0:T(8,128)(2,1)S(1)} %get-tuple-element.2), channel_id=1, source_target_pairs={{2,0},{3,1},{6,4},{7,5},{10,8},{11,9},{14,12},{15,13},{18,16},{19,... | collective-permute-start | bytes 776 | tf_op jit(solution)/shard_map/ppermute | solution.py:57
  3.6 4.3 %collective-permute-start = (bf16[8,16]{1,0:T(8,128)(2,1)S(1)}, bf16[8,16]{1,0:T(8,128)(2,1)S(1)}, u32[]{:S(2)}, u32[]{:S(2)}) collective-permute-start(bf16[8,16]{1,0:T(8,128)(2,1)S(1)} %get-tuple-element.3), channel_id=1, source_target_pairs={{0,2},{1,3},{4,6},{5,7},{8,10},{9,11},{12,14},{13,15},{16,18},{17,... | collective-permute-start | bytes 776 | tf_op jit(solution)/shard_map/ppermute | solution.py:56
  7.9 1.6 %copy-start = (bf16[2,512,1024]{2,1,0:T(8,128)(2,1)S(1)}, bf16[2,512,1024]{2,1,0:T(8,128)(2,1)}, u32[]{:S(2)}) copy-start(bf16[2,512,1024]{2,1,0:T(8,128)(2,1)} %constant.9.clone.tlow_ref) | copy-start | bytes 6291460
  9.5 1.6 %copy-start.1 = (bf16[2,512,1024]{2,1,0:T(8,128)(2,1)S(1)}, bf16[2,512,1024]{2,1,0:T(8,128)(2,1)}, u32[]{:S(2)}) copy-start(bf16[2,512,1024]{2,1,0:T(8,128)(2,1)} %constant.8.clone.thigh_ref) | copy-start | bytes 6291460
  11.1 0.9 %copy-start.4 = (s32[8,8192]{1,0:T(8,128)S(1)}, s32[8,8192]{1,0:T(8,128)}, u32[]{:S(2)}) copy-start(s32[8,8192]{1,0:T(8,128)} %flags_ref.1) | copy-start | bytes 786436
  12.0 0.9 %copy-start.5 = (s32[8,8192]{1,0:T(8,128)S(1)}, s32[8,8192]{1,0:T(8,128)}, u32[]{:S(2)}) copy-start(s32[8,8192]{1,0:T(8,128)} %pix_ref.1) | copy-start | bytes 786436
  13.0 0.9 %copy-start.6 = (bf16[8,8192]{1,0:T(8,128)(2,1)S(1)}, bf16[8,8192]{1,0:T(8,128)(2,1)}, u32[]{:S(2)}) copy-start(bf16[8,8192]{1,0:T(8,128)(2,1)} %ts_ref.1) | copy-start | bytes 393220
  13.9 0.8 %copy-start.7 = (s32[8192]{0:T(1024)S(1)}, s32[8192]{0:T(1024)}, u32[]{:S(2)}) copy-start(s32[8192]{0:T(1024)} %param.13) | copy-start | bytes 98308
  14.6 0.7 %copy-start.8 = (s32[8,16]{1,0:T(8,128)S(1)}, s32[8,16]{1,0:T(8,128)}, u32[]{:S(2)}) copy-start(s32[8,16]{1,0:T(8,128)} %tile_ref.1) | copy-start | bytes 1540
  15.3 0.7 %copy-start.9 = (f32[7,33]{1,0:T(8,128)S(1)}, f32[7,33]{1,0:T(8,128)}, u32[]{:S(2)}) copy-start(f32[7,33]{1,0:T(8,128)} %taps_ref.1) | copy-start | bytes 2776
  16.0 18.0 %copy-start.2 = (bf16[512,1024]{1,0:T(8,128)(2,1)S(1)}, bf16[512,1024]{1,0:T(8,128)(2,1)}, u32[]{:S(2)}) copy-start(bf16[512,1024]{1,0:T(8,128)(2,1)} %constant.11.clone.refs_2_) | copy-start | bytes 3145732
  16.0 18.0 %copy-start.3 = (bf16[512,1024]{1,0:T(8,128)(2,1)S(1)}, bf16[512,1024]{1,0:T(8,128)(2,1)}, u32[]{:S(2)}) copy-start(bf16[512,1024]{1,0:T(8,128)(2,1)} %constant.10.clone.refs_1_) | copy-start | bytes 3145732

commit v2 on v1

v2 whole, which is shorter than its diff:
```python
import math

import jax
import jax.numpy as jnp
import ml_dtypes
import numpy as np
from jax import lax
from jax.experimental import pallas as pl
from jax.experimental.pallas import tpu as pltpu
from jax.sharding import PartitionSpec as P

TILE = 128
MAPY = 2048
KY = 512
NANG = 8192
LANES = 128
CHUNK = 1024
HIGH = lax.Precision.HIGHEST
MESH = pl.DeviceIdType.MESH
NT = (((1,), (1,)), ((), ()))


def split_np(table):
    table = table.astype(np.float32)
    high = table.astype(ml_dtypes.bfloat16)
    low = (table - high.astype(np.float32)).astype(ml_dtypes.bfloat16)
    return high, low


def split(value):
    high = value.astype(jnp.bfloat16)
    return high, (value - high.astype(jnp.float32)).astype(jnp.bfloat16)


def row_tables(owners):
    kept = KY // owners
    ky = np.arange(KY).reshape(owners, 1, kept // 2, 2)
    ky = np.moveaxis(ky, 3, 0)
    y = np.arange(MAPY // 2)
    angle = (ky[..., None] * y % MAPY) * (2.0 * np.pi / MAPY)
    table = np.concatenate([np.cos(angle), -np.sin(angle)], axis=2)
    return split_np(table.reshape(2, KY, MAPY // 2))


def column_tables(length):
    pos = np.arange(length)
    angle = (pos[:, None] * pos[None, :] % length) * (2.0 * np.pi / length)
    table = np.concatenate([np.cos(angle), np.sin(angle)], axis=1)
    return split_np(table / math.sqrt(length * MAPY))


def rotation(kx, length, ky):
    fx = jnp.where(kx < length // 2, kx, kx - length).astype(jnp.float32)
    fy = ky.astype(jnp.float32)
    radius = jnp.maximum(fx * fx + fy * fy, 1.0)
    return (fx * fx - fy * fy) / radius, 2.0 * fx * fy / radius


def whole_kernel(
    sizes, direct,
    tile_ref, wafer_ref, angle_ref, ts_hbm, hwp_hbm, flags_hbm, pix_hbm, taps_hbm, thigh_hbm,
    tlow_hbm, *rest,
):
    n_det, n_tm, n_pol = sizes
    owners = n_det * n_tm * n_pol
    strips = n_tm * n_pol
    kept = KY // owners
    half = kept // 2
    length = strips * TILE
    if direct:
        whigh_hbm, wlow_hbm, e_ref, b_ref, *rest = rest
    else:
        out_ref, *rest = rest
    (ts, hwp_v, flags, pix, taps, t_high, t_low, in_sem, xs, cos_h, sin_h, q_s, u_s, rid_s, key_s,
     prev_s, last_s, sums_s, halo_send, halo_recv, *rest) = rest
    det_rows, time_len = ts.shape
    tap_count = taps.shape[1]
    width = (tap_count - 1) // 2
    block_count = tile_ref.shape[1]
    block_len = time_len // block_count
    tiles = MAPY // TILE
    det, tm, pol = lax.axis_index("det"), lax.axis_index("tm"), lax.axis_index("pol")
    me = (det * n_tm + tm) * n_pol + pol

    pairs = [(ts_hbm, ts), (hwp_hbm, hwp_v), (pix_hbm, pix), (taps_hbm, taps), (flags_hbm, flags),
             (thigh_hbm, t_high), (tlow_hbm, t_low)]
    if direct:
        w_high, w_low, spec_s, recv, ordered, send_sem, recv_sem = rest
        pairs += [(whigh_hbm, w_high), (wlow_hbm, w_low)]
    loads = [pltpu.make_async_copy(s, v, in_sem.at[i]) for i, (s, v) in enumerate(pairs)]
    for load in loads:
        load.start()

    xs[:, 0:LANES] = jnp.zeros((det_rows, LANES), jnp.float32)
    xs[:, LANES + time_len :] = jnp.zeros((det_rows, LANES), jnp.float32)
    barrier = pltpu.get_barrier_semaphore()
    has_left, has_right = tm > 0, tm < n_tm - 1
    if direct:
        order = [(s, x, c) for s in [2, 1, 3] + list(range(4, n_det)) if s < n_det
                 for x in range(n_tm) for c in range(n_pol)]
        order += [(0, x, c) for x in range(n_tm) for c in range(n_pol) if x or c]
        peers = [(lax.rem(det + s, n_det), lax.rem(tm + x, n_tm), lax.rem(pol + c, n_pol))
                 for s, x, c in order]
        for peer_det, peer_tm, peer_pol in peers:
            pl.semaphore_signal(
                barrier, inc=1, device_id={"det": peer_det, "tm": peer_tm, "pol": peer_pol},
                device_id_type=MESH,
            )
    else:
        @pl.when(has_left)
        def _():
            pl.semaphore_signal(barrier, inc=1, device_id={"tm": tm - 1}, device_id_type=MESH)

        @pl.when(has_right)
        def _():
            pl.semaphore_signal(barrier, inc=1, device_id={"tm": tm + 1}, device_id_type=MESH)

    def chain(b, last):
        last = list(last)
        for d in range(det_rows):
            tile = tile_ref[d, b]
            before = jnp.int32(0)
            for k in range(tiles):
                before = jnp.where(tile == k, last[k], before)
                last[k] = jnp.where(tile == k, b * det_rows + d + 1, last[k])
            prev_s[b * det_rows + d] = before
        return tuple(last)

    last = lax.fori_loop(0, block_count, chain, (jnp.int32(0),) * tiles)
    for k in range(tiles):
        last_s[k] = last[k]
    sums_s[0] = jnp.zeros(sums_s.shape[1:], jnp.float32)

    loads[0].wait()
    xs[:, LANES : LANES + time_len] = ts[...].astype(jnp.float32)
    if direct:
        pl.semaphore_wait(barrier, owners - 1)
    else:
        @pl.when(has_left)
        def _():
            pl.semaphore_wait(barrier, 1)

        @pl.when(has_right)
        def _():
            pl.semaphore_wait(barrier, 1)

    def halo(side):
        if side == 0:
            source, target, other = time_len, 0, lax.rem(tm + 1, n_tm)
        else:
            source, target, other = LANES, LANES + time_len, lax.rem(tm + n_tm - 1, n_tm)
        return pltpu.make_async_remote_copy(
            src_ref=xs.at[:, pl.ds(source, LANES)],
            dst_ref=xs.at[:, pl.ds(target, LANES)],
            send_sem=halo_send.at[side],
            recv_sem=halo_recv.at[side],
            device_id={"tm": other},
            device_id_type=MESH,
        )

    if n_tm > 1:
        @pl.when(has_right)
        def _():
            halo(0).start()

        @pl.when(has_left)
        def _():
            halo(1).start()

    loads[1].wait()
    hwp = (4 * hwp_v[...] % NANG).astype(jnp.float32) * (2.0 * math.pi / NANG)
    cos_h[...] = jnp.cos(hwp)
    sin_h[...] = jnp.sin(hwp)
    row = lax.broadcasted_iota(jnp.int32, (det_rows, LANES), 0)
    tap_row = lax.broadcasted_iota(jnp.int32, (det_rows, tap_count), 0)
    angle = jnp.zeros((det_rows, LANES), jnp.float32)
    wafer = jnp.zeros((det_rows, tap_count), jnp.int32)
    for d in range(det_rows):
        angle = jnp.where(row == d, angle_ref[d], angle)
        wafer = jnp.where(tap_row == d, wafer_ref[d], wafer)
    cos_a = jnp.cos(2.0 * angle)
    sin_a = jnp.sin(2.0 * angle)
    loads[2].wait()
    rid_s[...] = ((pix[...] >> 7) & (TILE // 2 - 1)).astype(jnp.float32)
    key_s[...] = (((pix[...] >> 13) << 7) + (pix[...] & (TILE - 1))).astype(jnp.float32)
    loads[3].wait()
    loads[4].wait()
    det_taps = jnp.zeros((det_rows, tap_count), jnp.float32)
    for w in range(taps.shape[0]):
        det_taps = det_taps + jnp.where(wafer == w, taps[w : w + 1, :], 0.0)

    chunk = min(CHUNK, time_len)
    chunks = time_len // chunk
    span = chunk + 2 * LANES
    per = chunk // LANES

    def filter_chunk(step):
        start = pl.multiple_of(step * chunk, chunk)
        base = xs[:, pl.ds(start, span)]
        total = jnp.zeros((det_rows, chunk), jnp.float32)
        for j in range(tap_count):
            moved = pltpu.roll(base, span - (LANES - width + j), 1)
            total = total + det_taps[:, j : j + 1] * moved[:, :chunk]
        flagged = total * flags[:, pl.ds(start, chunk)].astype(jnp.float32)
        rows = pl.ds(pl.multiple_of(step * per, per), per)
        ch = cos_h[rows, :]
        sh = sin_h[rows, :]
        for k in range(per):
            lanes = pl.ds(pl.multiple_of(start + k * LANES, LANES), LANES)
            part = flagged[:, k * LANES : (k + 1) * LANES]
            c = ch[k : k + 1, :]
            s = sh[k : k + 1, :]
            q_s[:, lanes] = part * (c * cos_a + s * sin_a)
            u_s[:, lanes] = part * (s * cos_a - c * sin_a)

    @pl.loop(1, chunks - 1)
    def _(step):
        filter_chunk(step)

    if n_tm > 1:
        @pl.when(has_left)
        def _():
            halo(0).wait_recv()
            halo(1).wait_send()

        @pl.when(has_right)
        def _():
            halo(1).wait_recv()
            halo(0).wait_send()

    @pl.loop(0, 2)
    def _(side):
        filter_chunk(side * (chunks - 1))

    sub = 16
    side = lax.broadcasted_iota(jnp.int32, (sub, block_len), 0).astype(jnp.float32)
    zero = jnp.zeros((sub, block_len), jnp.bfloat16)
    ids = [(side + float(g * sub)).astype(jnp.bfloat16) for g in range(TILE // 2 // sub)]
    lane = lax.broadcasted_iota(jnp.int32, (block_len, TILE), 1).astype(jnp.float32)
    keys = [lane.astype(jnp.bfloat16), (lane + float(TILE)).astype(jnp.bfloat16)]
    zeros = jnp.zeros((block_len, TILE), jnp.bfloat16)
    ones = jnp.ones((block_len, TILE), jnp.bfloat16)

    def spread(value):
        return jnp.broadcast_to(value, (sub, block_len)).astype(jnp.bfloat16)

    @pl.loop(0, block_count)
    def _(b):
        lanes = pl.ds(pl.multiple_of(b * block_len, block_len), block_len)
        turned = jnp.transpose(key_s[:, lanes])
        for d in range(det_rows):
            row_id = spread(rid_s[d : d + 1, lanes])
            qv = spread(q_s[d : d + 1, lanes])
            uv = spread(u_s[d : d + 1, lanes])
            hits = [row_id == i for i in ids]
            weighted = jnp.concatenate(
                [jnp.where(h, qv, zero) for h in hits] + [jnp.where(h, uv, zero) for h in hits],
                axis=0,
            )
            key = jnp.broadcast_to(turned[:, d : d + 1], (block_len, TILE)).astype(jnp.bfloat16)
            hot = jnp.concatenate([jnp.where(key == i, ones, zeros) for i in keys], axis=1)
            sums = jnp.dot(weighted, hot, preferred_element_type=jnp.float32)
            slot = b * det_rows + d
            sums_s[slot + 1] = sums_s[prev_s[slot]] + sums

    def tile_rows(k):
        found = sums_s[last_s[k]]
        return jnp.concatenate(
            [found[c * TILE // 2 : (c + 1) * TILE // 2, m * TILE : (m + 1) * TILE]
             for c in range(2) for m in range(2)], axis=0)

    first = jnp.concatenate([tile_rows(k) for k in range(tiles // 2)], axis=1)
    second = jnp.concatenate([tile_rows(k) for k in range(tiles // 2, tiles)], axis=1)
    for load in loads[5:]:
        load.wait()
    copies = [[], []]
    for parity in range(2):
        folded = first + second if parity == 0 else first - second
        f_high, f_low = split(folded)
        acc = lax.dot_general(t_high[parity], f_high, NT, preferred_element_type=jnp.float32)
        acc = acc + lax.dot_general(t_high[parity], f_low, NT, preferred_element_type=jnp.float32)
        acc = acc + lax.dot_general(t_low[parity], f_high, NT, preferred_element_type=jnp.float32)
        for c in range(2):
            piece = acc[:, c * TILE : (c + 1) * TILE].astype(jnp.bfloat16)
            if direct:
                spec_s[parity, c] = piece
            else:
                out_ref[2 * parity + c] = piece
        if not direct:
            continue
        for at, (peer_det, peer_tm, peer_pol) in enumerate(peers):
            peer = (peer_det * n_tm + peer_tm) * n_pol + peer_pol
            copy = pltpu.make_async_remote_copy(
                src_ref=spec_s.at[parity, :, pl.ds(pl.multiple_of(peer * kept, kept), kept), :],
                dst_ref=recv.at[me, parity],
                send_sem=send_sem.at[parity, at],
                recv_sem=recv_sem.at[parity, at],
                device_id={"det": peer_det, "tm": peer_tm, "pol": peer_pol},
                device_id_type=MESH,
            )
            copy.start()
            copies[parity].append(copy)
    if not direct:
        return

    own = pl.ds(pl.multiple_of(me * kept, kept), kept)
    for parity in range(2):
        recv[me, parity] = spec_s[parity, :, own, :]
    kx = lax.broadcasted_iota(jnp.int32, (kept, length), 1)
    ky = me * kept + lax.broadcasted_iota(jnp.int32, (kept, length), 0)
    cosine, sine = rotation(kx, length, ky)
    for parity in range(2):
        for copy in copies[parity]:
            copy.wait_recv()
        for strip in range(strips):
            total = recv[strip, parity].astype(jnp.float32)
            for d in range(1, n_det):
                total = total + recv[d * strips + strip, parity].astype(jnp.float32)
            for c in range(2):
                for part in range(2):
                    ordered[strip, c, part, pl.ds(parity, half, stride=2), :] = total[
                        c, part * half : (part + 1) * half
                    ]
    columns = [ordered[strip].reshape(4 * kept, TILE) for strip in range(strips)]
    x_high, x_low = split(jnp.concatenate(columns, axis=1))
    acc = jnp.dot(x_high, w_high[...], preferred_element_type=jnp.float32)
    acc = acc + jnp.dot(x_low, w_high[...], preferred_element_type=jnp.float32)
    acc = acc + jnp.dot(x_high, w_low[...], preferred_element_type=jnp.float32)
    real, imag = [], []
    for c in range(2):
        re_rows = slice(2 * c * kept, (2 * c + 1) * kept)
        im_rows = slice((2 * c + 1) * kept, (2 * c + 2) * kept)
        real.append(acc[re_rows, :length] + acc[im_rows, length:])
        imag.append(acc[im_rows, :length] - acc[re_rows, length:])
    e_ref[0] = cosine * real[0] + sine * real[1]
    e_ref[1] = cosine * imag[0] + sine * imag[1]
    b_ref[0] = cosine * real[1] - sine * real[0]
    b_ref[1] = cosine * imag[1] - sine * imag[0]
    for parity in range(2):
        for copy in copies[parity]:
            copy.wait_send()


def run_whole(sizes, direct, timestream, hwp_index, flags, pixel_index, tile_index, wafer, taps, angle):
    det_rows, time_len = timestream.shape
    owners = math.prod(sizes)
    strips = sizes[1] * sizes[2]
    kept = KY // owners
    length = strips * TILE
    blocks = tile_index.size
    tables = [jnp.asarray(t) for t in row_tables(owners)]
    if direct:
        tables += [jnp.asarray(t) for t in column_tables(length)]
    hwp_grid = hwp_index.reshape(time_len // LANES, LANES)
    loaded = [timestream, hwp_grid, flags, pixel_index, taps] + tables[:2]
    smem = pl.BlockSpec(memory_space=pltpu.SMEM)
    vmem = pl.BlockSpec(memory_space=pltpu.VMEM)
    hbm = pl.BlockSpec(memory_space=pl.ANY)
    wide = pltpu.VMEM((det_rows, time_len), jnp.float32)
    grid = pltpu.VMEM((time_len // LANES, LANES), jnp.float32)
    scratch = [pltpu.VMEM(x.shape, x.dtype) for x in loaded]
    scratch += [
        pltpu.SemaphoreType.DMA((9,)),
        pltpu.VMEM((det_rows, time_len + 2 * LANES), jnp.float32),
        grid, grid, wide, wide, wide, wide,
        pltpu.SMEM((blocks,), jnp.int32),
        pltpu.SMEM((MAPY // TILE,), jnp.int32),
        pltpu.VMEM((blocks + 1, TILE, 2 * TILE), jnp.float32),
        pltpu.SemaphoreType.DMA((2,)),
        pltpu.SemaphoreType.DMA((2,)),
    ]
    if direct:
        scratch += [pltpu.VMEM(x.shape, x.dtype) for x in tables[2:]]
        scratch += [
            pltpu.VMEM((2, 2, KY, TILE), jnp.bfloat16),
            pltpu.VMEM((owners, 2, 2, kept, TILE), jnp.bfloat16),
            pltpu.VMEM((strips, 2, 2, kept, TILE), jnp.float32),
            pltpu.SemaphoreType.DMA((2, owners)),
            pltpu.SemaphoreType.DMA((2, owners)),
        ]
        shape = jax.ShapeDtypeStruct((2, kept, length), jnp.float32)
        out_shape, out_specs = (shape, shape), (vmem, vmem)
    else:
        out_shape, out_specs = jax.ShapeDtypeStruct((4, KY, TILE), jnp.bfloat16), vmem

    def kernel(*refs):
        whole_kernel(sizes, direct, *refs)

    return pl.pallas_call(
        kernel,
        out_shape=out_shape,
        in_specs=[smem] * 3 + [hbm] * (5 + len(tables)),
        out_specs=out_specs,
        scratch_shapes=scratch,
        compiler_params=pltpu.CompilerParams(
            collective_id=0, has_side_effects=True, vmem_limit_bytes=56 * 2**20
        ),
        name="map_to_modes",
    )(tile_index, wafer, angle, timestream, hwp_grid, flags, pixel_index, taps, *tables)


def twiddle_table(first, second, length):
    return (first * second % length).astype(jnp.float32) * (2.0 * math.pi / length)


def transform_columns(real_in, imag_in):
    lead, kept, length = real_in.shape
    outer = TILE
    inner = length // outer
    real_grid = real_in.reshape(lead, kept, outer, inner)
    imag_grid = imag_in.reshape(lead, kept, outer, inner)
    outer_pos = jnp.arange(outer, dtype=jnp.int32)
    inner_pos = jnp.arange(inner, dtype=jnp.int32)
    first_angle = twiddle_table(outer_pos[:, None], outer_pos[None, :], outer)
    first_cos = jnp.cos(first_angle)
    first_sin = jnp.sin(first_angle)
    section_real = jnp.einsum("ckab,ad->ckdb", real_grid, first_cos, precision=HIGH) + jnp.einsum(
        "ckab,ad->ckdb", imag_grid, first_sin, precision=HIGH
    )
    section_imag = jnp.einsum("ckab,ad->ckdb", imag_grid, first_cos, precision=HIGH) - jnp.einsum(
        "ckab,ad->ckdb", real_grid, first_sin, precision=HIGH
    )
    mid_angle = twiddle_table(outer_pos[:, None], inner_pos[None, :], length)
    mid_cos = jnp.cos(mid_angle)
    mid_sin = jnp.sin(mid_angle)
    turned_real = section_real * mid_cos + section_imag * mid_sin
    turned_imag = section_imag * mid_cos - section_real * mid_sin
    last_angle = twiddle_table(inner_pos[:, None], inner_pos[None, :], inner)
    last_cos = jnp.cos(last_angle)
    last_sin = jnp.sin(last_angle)
    final_real = jnp.einsum("ckdb,be->cked", turned_real, last_cos, precision=HIGH) + jnp.einsum(
        "ckdb,be->cked", turned_imag, last_sin, precision=HIGH
    )
    final_imag = jnp.einsum("ckdb,be->cked", turned_imag, last_cos, precision=HIGH) - jnp.einsum(
        "ckdb,be->cked", turned_real, last_sin, precision=HIGH
    )
    return (final_real.reshape(lead, kept, length), final_imag.reshape(lead, kept, length))


def exchange_many(spec, sizes):
    n_det, n_tm, n_pol = sizes
    owners = math.prod(sizes)
    kept = KY // owners
    half = kept // 2
    strips = n_tm * n_pol
    length = strips * TILE
    pieces = spec.reshape(2, 2, owners, 2, half, TILE)
    moved = lax.all_to_all(pieces, ("det", "tm", "pol"), split_axis=2, concat_axis=2, tiled=True)
    summed = jnp.sum(moved.reshape(2, 2, n_det, strips, 2, half, TILE).astype(jnp.float32), axis=2)
    columns = jnp.transpose(summed, (3, 1, 4, 0, 2, 5)).reshape(2, 2, kept, length)
    final_real, final_imag = transform_columns(columns[0], columns[1])
    norm_scale = 1.0 / math.sqrt(length * MAPY)
    real = final_real * norm_scale
    imag = final_imag * norm_scale
    position = (lax.axis_index("det") * n_tm + lax.axis_index("tm")) * n_pol + lax.axis_index("pol")
    cosine, sine = rotation(
        jnp.arange(length, dtype=jnp.int32)[None, :],
        length,
        (position * kept + jnp.arange(kept, dtype=jnp.int32))[:, None],
    )
    return (
        jnp.stack([cosine * real[0] + sine * real[1], cosine * imag[0] + sine * imag[1]]),
        jnp.stack([cosine * real[1] - sine * real[0], cosine * imag[1] - sine * imag[0]]),
    )


def solution(mesh):
    sizes = (mesh.shape["det"], mesh.shape["tm"], mesh.shape["pol"])
    direct = KY // math.prod(sizes) % 32 == 0

    def body(*args):
        found = run_whole(sizes, direct, *args)
        return found if direct else exchange_many(found, sizes)

    in_specs = (
        P(("group", "det", "pol"), "tm"),
        P(("group", "tm")),
        P(("group", "det", "pol"), "tm"),
        P(("group", "det", "pol"), "tm"),
        P(("group", "det", "pol"), "tm"),
        P(("group", "det", "pol")),
        P(),
        P(("group", "det", "pol")),
    )
    out_specs = (
        P(None, ("group", "det", "tm", "pol"), None),
        P(None, ("group", "det", "tm", "pol"), None),
    )
    return jax.shard_map(body, mesh=mesh, in_specs=in_specs, out_specs=out_specs, check_vma=False)
```

time: 54.9 us -> 43.9 us (0.80)
  the two profiles are of different devices: /device:TPU:11 before, /device:TPU:0 now
where the time goes in v2:
time: 43.9 us; the launch traced here: 43.7 us
  Pallas kernels  40 us (91%)
  local copies, waits for them, and re-layouts  3.14 us (7%)
  between operations  0.64 us (1%)
    pallas_call x1, Pallas kernels, run_whole(): pl.pallas_call(kernel, out_shape=out_shape, in_specs=[smem] * 3 + [hbm] *...  40 us
    unnamed x2, local copies, waits for them, and re-layouts  3.14 us

profile of v2, /device:TPU:0, one launch (start us, length us, event | category | flops | bytes accessed | tf_op | source)
XLA Modules:
  0.0 43.7 jit_solution(6045840484333701450)
XLA Ops:
  0.6 40.0 %map_to_modes.1 = (f32[2,32,512]{2,1,0:T(8,128)}, f32[2,32,512]{2,1,0:T(8,128)}) custom-call(s32[8,16]{1,0:T(8,128)} %refs_0_.1, s32[8]{0:T(128)} %refs_1_.1, f32[8]{0:T(128)} %refs_2_.1, bf16[8,8192]{1,0:T(8,128)(2,1)} %refs_3_.1, s32[64,128]{1,0:T(8,128)} %bitcast.1, s32[8,8192]{1,0:T(8,128)} %refs_5_.1, s32[8,8192]{1,0:T(8,128)} %refs_6_.1, ...), custom_call_target="tpu_custom_call" | custom-call | tf_op jit(solution)/shard_map/map_to_modes/pallas_call | solution.py:389
  40.6 1.6 %copy.16 = f32[2,32,512]{2,1,0:T(8,128)} copy(f32[2,32,512]{2,1,0:T(8,128)} %get-tuple-element.4) | data formatting | bytes 262144
  42.2 1.6 %copy.17 = f32[2,32,512]{2,1,0:T(8,128)} copy(f32[2,32,512]{2,1,0:T(8,128)} %get-tuple-element.5) | data formatting | bytes 262144

commit v3 on v2

--- a/solution.py
+++ b/solution.py
@@ -68,7 +68,7 @@
     half = kept // 2
     length = strips * TILE
     if direct:
-        whigh_hbm, wlow_hbm, e_ref, b_ref, *rest = rest
+        whigh_hbm, wlow_hbm, modes_ref, *rest = rest
     else:
         out_ref, *rest = rest
     (ts, hwp_v, flags, pix, taps, t_high, t_low, in_sem, xs, cos_h, sin_h, q_s, u_s, rid_s, key_s,
@@ -85,7 +85,7 @@
     pairs = [(ts_hbm, ts), (hwp_hbm, hwp_v), (pix_hbm, pix), (taps_hbm, taps), (flags_hbm, flags),
              (thigh_hbm, t_high), (tlow_hbm, t_low)]
     if direct:
-        w_high, w_low, spec_s, recv, ordered, send_sem, recv_sem = rest
+        w_high, w_low, spec_s, recv, passed, joined, ordered, send_sem, recv_sem, chunk_send, chunk_recv = rest
         pairs += [(whigh_hbm, w_high), (wlow_hbm, w_low)]
     loads = [pltpu.make_async_copy(s, v, in_sem.at[i]) for i, (s, v) in enumerate(pairs)]
     for load in loads:
@@ -96,16 +96,13 @@
     barrier = pltpu.get_barrier_semaphore()
     has_left, has_right = tm > 0, tm < n_tm - 1
     if direct:
-        order = [(s, x, c) for s in [2, 1, 3] + list(range(4, n_det)) if s < n_det
+        turns = [(lax.rem(tm + x, n_tm), lax.rem(pol + c, n_pol))
                  for x in range(n_tm) for c in range(n_pol)]
-        order += [(0, x, c) for x in range(n_tm) for c in range(n_pol) if x or c]
-        peers = [(lax.rem(det + s, n_det), lax.rem(tm + x, n_tm), lax.rem(pol + c, n_pol))
-                 for s, x, c in order]
-        for peer_det, peer_tm, peer_pol in peers:
-            pl.semaphore_signal(
-                barrier, inc=1, device_id={"det": peer_det, "tm": peer_tm, "pol": peer_pol},
-                device_id_type=MESH,
-            )
+        for s in range(n_det):
+            for r, (peer_tm, peer_pol) in enumerate(turns):
+                if s or r:
+                    peer = {"det": lax.rem(det + s, n_det), "tm": peer_tm, "pol": peer_pol}
+                    pl.semaphore_signal(barrier, inc=1, device_id=peer, device_id_type=MESH)
     else:
         @pl.when(has_left)
         def _():
@@ -273,7 +270,51 @@
     second = jnp.concatenate([tile_rows(k) for k in range(tiles // 2, tiles)], axis=1)
     for load in loads[5:]:
         load.wait()
-    copies = [[], []]
+    if direct:
+        strip_at = tm * n_pol + pol
+        near = det // 2 * 2 + 1 - lax.rem(det, 2)
+        left = det < 2
+        edge = (det == 0) | (det == n_det - 1)
+        inner = (det == 1) | (det == 2)
+        far = [jnp.where(left, 3 - h, h) for h in range(2)]
+
+        def piece_rows(peer_det, r):
+            peer = (peer_det * n_tm + turns[r][0]) * n_pol + turns[r][1]
+            return pl.ds(pl.multiple_of(peer * kept, kept), kept)
+
+        def send(kind, r, parity, h=0):
+            peer_det = (det, near, far[h])[kind]
+            if kind < 2:
+                source = spec_s.at[parity, :, piece_rows(peer_det, r), :]
+            else:
+                peer = turns[r][0] * n_pol + turns[r][1]
+                source = joined.at[parity, h, :, pl.ds(pl.multiple_of(peer * kept, kept), kept), :]
+            return pltpu.make_async_remote_copy(
+                src_ref=source,
+                dst_ref=recv.at[kind, strip_at, parity],
+                send_sem=send_sem.at[kind + h, r, parity],
+                recv_sem=recv_sem.at[kind, r, parity],
+                device_id={"det": peer_det, "tm": turns[r][0], "pol": turns[r][1]},
+                device_id_type=MESH,
+            )
+
+        def send_chunk(parity, h):
+            rows = pl.ds(pl.multiple_of(far[h] * strips * kept, strips * kept), strips * kept)
+            return pltpu.make_async_remote_copy(
+                src_ref=spec_s.at[parity, :, rows, :],
+                dst_ref=passed.at[parity, h],
+                send_sem=chunk_send.at[parity, h],
+                recv_sem=chunk_recv.at[parity, h],
+                device_id={"det": near},
+                device_id_type=MESH,
+            )
+
+        def send_near(parity):
+            for r in range(strips):
+                send(1, r, parity).start()
+            for r in range(1, strips):
+                send(0, r, parity).start()
+
     for parity in range(2):
         folded = first + second if parity == 0 else first - second
         f_high, f_low = split(folded)
@@ -286,36 +327,47 @@
                 spec_s[parity, c] = piece
             else:
                 out_ref[2 * parity + c] = piece
-        if not direct:
-            continue
-        for at, (peer_det, peer_tm, peer_pol) in enumerate(peers):
-            peer = (peer_det * n_tm + peer_tm) * n_pol + peer_pol
-            copy = pltpu.make_async_remote_copy(
-                src_ref=spec_s.at[parity, :, pl.ds(pl.multiple_of(peer * kept, kept), kept), :],
-                dst_ref=recv.at[me, parity],
-                send_sem=send_sem.at[parity, at],
-                recv_sem=recv_sem.at[parity, at],
-                device_id={"det": peer_det, "tm": peer_tm, "pol": peer_pol},
-                device_id_type=MESH,
-            )
-            copy.start()
-            copies[parity].append(copy)
+        if direct:
+            @pl.when(edge)
+            def _():
+                for h in range(2):
+                    send_chunk(parity, h).start()
+
+            @pl.when(inner)
+            def _():
+                send_near(parity)
     if not direct:
         return
 
+    @pl.when(edge)
+    def _():
+        for parity in range(2):
+            send_near(parity)
+
+    @pl.when(inner)
+    def _():
+        for parity in range(2):
+            for h in range(2):
+                send_chunk(parity, h).wait_recv()
+                rows = pl.ds(pl.multiple_of(far[h] * strips * kept, strips * kept), strips * kept)
+                both = passed[parity, h].astype(jnp.float32) + spec_s[parity, :, rows, :].astype(
+                    jnp.float32
+                )
+                joined[parity, h] = both.astype(jnp.bfloat16)
+                for r in range(strips):
+                    send(2, r, parity, h).start()
+
     own = pl.ds(pl.multiple_of(me * kept, kept), kept)
     for parity in range(2):
-        recv[me, parity] = spec_s[parity, :, own, :]
-    kx = lax.broadcasted_iota(jnp.int32, (kept, length), 1)
-    ky = me * kept + lax.broadcasted_iota(jnp.int32, (kept, length), 0)
-    cosine, sine = rotation(kx, length, ky)
+        recv[0, strip_at, parity] = spec_s[parity, :, own, :]
     for parity in range(2):
-        for copy in copies[parity]:
-            copy.wait_recv()
+        for kind in range(3):
+            for r in range(0 if kind else 1, strips):
+                send(kind, r, parity).wait_recv()
         for strip in range(strips):
-            total = recv[strip, parity].astype(jnp.float32)
-            for d in range(1, n_det):
-                total = total + recv[d * strips + strip, parity].astype(jnp.float32)
+            total = recv[0, strip, parity].astype(jnp.float32)
+            for kind in range(1, 3):
+                total = total + recv[kind, strip, parity].astype(jnp.float32)
             for c in range(2):
                 for part in range(2):
                     ordered[strip, c, part, pl.ds(parity, half, stride=2), :] = total[
@@ -332,13 +384,26 @@
         im_rows = slice((2 * c + 1) * kept, (2 * c + 2) * kept)
         real.append(acc[re_rows, :length] + acc[im_rows, length:])
         imag.append(acc[im_rows, :length] - acc[re_rows, length:])
-    e_ref[0] = cosine * real[0] + sine * real[1]
-    e_ref[1] = cosine * imag[0] + sine * imag[1]
-    b_ref[0] = cosine * real[1] - sine * real[0]
-    b_ref[1] = cosine * imag[1] - sine * imag[0]
+    for c in range(2):
+        modes_ref[c, 0] = real[c]
+        modes_ref[c, 1] = imag[c]
     for parity in range(2):
-        for copy in copies[parity]:
-            copy.wait_send()
+        for kind in range(2):
+            for r in range(0 if kind else 1, strips):
+                send(kind, r, parity).wait_send()
+
+    @pl.when(edge)
+    def _():
+        for parity in range(2):
+            for h in range(2):
+                send_chunk(parity, h).wait_send()
+
+    @pl.when(inner)
+    def _():
+        for parity in range(2):
+            for h in range(2):
+                for r in range(strips):
+                    send(2, r, parity, h).wait_send()
 
 
 def run_whole(sizes, direct, timestream, hwp_index, flags, pixel_index, tile_index, wafer, taps, angle):
@@ -373,13 +438,16 @@
         scratch += [pltpu.VMEM(x.shape, x.dtype) for x in tables[2:]]
         scratch += [
             pltpu.VMEM((2, 2, KY, TILE), jnp.bfloat16),
-            pltpu.VMEM((owners, 2, 2, kept, TILE), jnp.bfloat16),
+            pltpu.VMEM((3, strips, 2, 2, kept, TILE), jnp.bfloat16),
+            pltpu.VMEM((2, 2, 2, strips * kept, TILE), jnp.bfloat16),
+            pltpu.VMEM((2, 2, 2, strips * kept, TILE), jnp.bfloat16),
             pltpu.VMEM((strips, 2, 2, kept, TILE), jnp.float32),
-            pltpu.SemaphoreType.DMA((2, owners)),
-            pltpu.SemaphoreType.DMA((2, owners)),
+            pltpu.SemaphoreType.DMA((4, strips, 2)),
+            pltpu.SemaphoreType.DMA((3, strips, 2)),
+            pltpu.SemaphoreType.DMA((2, 2)),
+            pltpu.SemaphoreType.DMA((2, 2)),
         ]
-        shape = jax.ShapeDtypeStruct((2, kept, length), jnp.float32)
-        out_shape, out_specs = (shape, shape), (vmem, vmem)
+        out_shape, out_specs = jax.ShapeDtypeStruct((2, 2, kept, length), jnp.float32), vmem
     else:
         out_shape, out_specs = jax.ShapeDtypeStruct((4, KY, TILE), jnp.bfloat16), vmem
 
@@ -466,11 +534,19 @@
 
 def solution(mesh):
     sizes = (mesh.shape["det"], mesh.shape["tm"], mesh.shape["pol"])
-    direct = KY // math.prod(sizes) % 32 == 0
+    direct = sizes[0] == 4 and KY // math.prod(sizes) % 32 == 0
 
     def body(*args):
         found = run_whole(sizes, direct, *args)
-        return found if direct else exchange_many(found, sizes)
+        if not direct:
+            return exchange_many(found, sizes)
+        _, _, kept, length = found.shape
+        at = (lax.axis_index("det") * sizes[1] + lax.axis_index("tm")) * sizes[2]
+        at = (at + lax.axis_index("pol")) * kept
+        shape = (2, kept, length)
+        kx = lax.broadcasted_iota(jnp.int32, shape, 2)
+        cosine, sine = rotation(kx, length, at + lax.broadcasted_iota(jnp.int32, shape, 1))
+        return cosine * found[0] + sine * found[1], cosine * found[1] - sine * found[0]
 
     in_specs = (
         P(("group", "det", "pol"), "tm"),

time: 43.9 us -> 40.9 us (0.932)
  local copies, waits for them, and re-layouts: 3.14 us -> 0 us
  other arithmetic: 0 us -> 1.8 us
  Pallas kernels: 40 us -> 38.2 us
    unnamed x2 -> x0, local copies, waits for them, and re-layouts: 3.14 us -> none
    sub x0 -> x2, other arithmetic: none -> 1.79 us  [the longest x1 1.78 us: body(): cosine * found[1] - sine * found[0]]
    pallas_call x1, Pallas kernels: 40 us -> 38.2 us  [run_whole(): pl.pallas_call(kernel, out_shape=out_shape, in_specs=[smem] * 3 + [hbm] *...]
where the time goes in v3:
time: 40.9 us; the launch traced here: 40.7 us
  Pallas kernels  38.2 us (93%)
  other arithmetic  1.8 us (4%)
  between operations  0.66 us (2%)
    pallas_call x1, Pallas kernels, run_whole(): pl.pallas_call(kernel, out_shape=out_shape, in_specs=[smem] * 3 + [hbm] *...  38.2 us
    sub x1, other arithmetic, body(): cosine * found[1] - sine * found[0]  1.78 us

profile of v3, /device:TPU:0, one launch (start us, length us, event | category | flops | bytes accessed | tf_op | source)
XLA Modules:
  0.0 40.7 jit_solution(5035550171694963274)
XLA Ops:
  0.7 38.2 %map_to_modes.1 = f32[2,2,32,512]{3,2,1,0:T(8,128)} custom-call(s32[8,16]{1,0:T(8,128)} %refs_0_.1, s32[8]{0:T(128)} %refs_1_.1, f32[8]{0:T(128)} %refs_2_.1, bf16[8,8192]{1,0:T(8,128)(2,1)} %refs_3_.1, s32[64,128]{1,0:T(8,128)} %bitcast.15, s32[8,8192]{1,0:T(8,128)} %refs_5_.1, s32[8,8192]{1,0:T(8,128)} %refs_6_.1, f32[7,33]{1,0:T(8,128)} %refs_7_.1, ...), custom_call_target="tpu_custom_call" | custom-call | tf_op jit(solution)/shard_map/map_to_modes/pallas_call | solution.py:457
  38.9 1.8 %fusion.1 = (f32[2,32,512]{2,1,0:T(8,128)}, f32[2,32,512]{2,1,0:T(8,128)}) fusion(f32[2,2,32,512]{3,2,1,0:T(8,128)} %map_to_modes.1, f32[32]{0:T(128)S(1)} %get-tuple-element.4, f32[32]{0:T(128)S(1)} %get-tuple-element.5, s32[512]{0:T(512)S(1)} %iota_add_fusion, pred[512]{0:T(512)(128)(4,1)S(1)} %iota_compare_fusion), kind=kLoop, calls=%fused_computation.3 | loop fusion | flops 491520 | bytes 527104 | tf_op jit(solution)/shard_map/sub | solution.py:549
  (3 shorter events, 0.0 us)

commit v4 on v3

--- a/solution.py
+++ b/solution.py
@@ -315,34 +315,33 @@
             for r in range(1, strips):
                 send(0, r, parity).start()
 
-    for parity in range(2):
-        folded = first + second if parity == 0 else first - second
-        f_high, f_low = split(folded)
-        acc = lax.dot_general(t_high[parity], f_high, NT, preferred_element_type=jnp.float32)
-        acc = acc + lax.dot_general(t_high[parity], f_low, NT, preferred_element_type=jnp.float32)
-        acc = acc + lax.dot_general(t_low[parity], f_high, NT, preferred_element_type=jnp.float32)
-        for c in range(2):
-            piece = acc[:, c * TILE : (c + 1) * TILE].astype(jnp.bfloat16)
-            if direct:
-                spec_s[parity, c] = piece
-            else:
-                out_ref[2 * parity + c] = piece
-        if direct:
-            @pl.when(edge)
-            def _():
-                for h in range(2):
-                    send_chunk(parity, h).start()
-
-            @pl.when(inner)
-            def _():
+    folds = [split(first + second), split(first - second)]
+    starts = [jnp.where(left, KY // 2, 0), jnp.where(left, 0, KY // 2)] if direct else [0]
+    count = KY // len(starts)
+    for at, start in enumerate(starts):
+        rows = pl.ds(pl.multiple_of(start, count), count)
+        for parity, (f_high, f_low) in enumerate(folds):
+            table = t_high[parity, rows, :]
+            acc = lax.dot_general(table, f_high, NT, preferred_element_type=jnp.float32)
+            acc = acc + lax.dot_general(table, f_low, NT, preferred_element_type=jnp.float32)
+            acc = acc + lax.dot_general(
+                t_low[parity, rows, :], f_high, NT, preferred_element_type=jnp.float32
+            )
+            for c in range(2):
+                piece = acc[:, c * TILE : (c + 1) * TILE].astype(jnp.bfloat16)
+                if direct:
+                    spec_s[parity, c, rows, :] = piece
+                else:
+                    out_ref[2 * parity + c] = piece
+            if direct and at:
                 send_near(parity)
+            elif direct:
+                @pl.when(edge)
+                def _():
+                    for h in range(2):
+                        send_chunk(parity, h).start()
     if not direct:
         return
-
-    @pl.when(edge)
-    def _():
-        for parity in range(2):
-            send_near(parity)
 
     @pl.when(inner)
     def _():

time: 40.9 us -> 40.4 us (0.988)
  Pallas kernels: 38.2 us -> 37.7 us
    pallas_call x1, Pallas kernels: 38.2 us -> 37.7 us  [run_whole(): pl.pallas_call(kernel, out_shape=out_shape, in_specs=[smem] * 3 + [hbm] *...]
where the time goes in v4:
time: 40.4 us; the launch traced here: 40.2 us
  Pallas kernels  37.7 us (93%)
  other arithmetic  1.8 us (4%)
  between operations  0.66 us (2%)
    pallas_call x1, Pallas kernels, run_whole(): pl.pallas_call(kernel, out_shape=out_shape, in_specs=[smem] * 3 + [hbm] *...  37.7 us
    sub x1, other arithmetic, body(): cosine * found[1] - sine * found[0]  1.78 us

profile of v4, /device:TPU:0, one launch (start us, length us, event | category | flops | bytes accessed | tf_op | source)
XLA Modules:
  0.0 40.2 jit_solution(1693072566300479640)
XLA Ops:
  0.7 37.7 %map_to_modes.1 = f32[2,2,32,512]{3,2,1,0:T(8,128)} custom-call(s32[8,16]{1,0:T(8,128)} %refs_0_.1, s32[8]{0:T(128)} %refs_1_.1, f32[8]{0:T(128)} %refs_2_.1, bf16[8,8192]{1,0:T(8,128)(2,1)} %refs_3_.1, s32[64,128]{1,0:T(8,128)} %bitcast.15, s32[8,8192]{1,0:T(8,128)} %refs_5_.1, s32[8,8192]{1,0:T(8,128)} %refs_6_.1, f32[7,33]{1,0:T(8,128)} %refs_7_.1, ...), custom_call_target="tpu_custom_call" | custom-call | tf_op jit(solution)/shard_map/map_to_modes/pallas_call | solution.py:456
  38.4 1.8 %fusion.1 = (f32[2,32,512]{2,1,0:T(8,128)}, f32[2,32,512]{2,1,0:T(8,128)}) fusion(f32[2,2,32,512]{3,2,1,0:T(8,128)} %map_to_modes.1, f32[32]{0:T(128)S(1)} %get-tuple-element.4, f32[32]{0:T(128)S(1)} %get-tuple-element.5, s32[512]{0:T(512)S(1)} %iota_add_fusion, pred[512]{0:T(512)(128)(4,1)S(1)} %iota_compare_fusion), kind=kLoop, calls=%fused_computation.3 | loop fusion | flops 491520 | bytes 527104 | tf_op jit(solution)/shard_map/sub | solution.py:548
  (3 shorter events, 0.0 us)

commit v5 on v4

--- a/solution.py
+++ b/solution.py
@@ -282,29 +282,29 @@
             peer = (peer_det * n_tm + turns[r][0]) * n_pol + turns[r][1]
             return pl.ds(pl.multiple_of(peer * kept, kept), kept)
 
-        def send(kind, r, parity, h=0):
+        def send(kind, r, parity, h=0, c=0):
             peer_det = (det, near, far[h])[kind]
             if kind < 2:
                 source = spec_s.at[parity, :, piece_rows(peer_det, r), :]
             else:
                 peer = turns[r][0] * n_pol + turns[r][1]
-                source = joined.at[parity, h, :, pl.ds(pl.multiple_of(peer * kept, kept), kept), :]
+                source = joined.at[parity, h, c, pl.ds(pl.multiple_of(peer * kept, kept), kept), :]
             return pltpu.make_async_remote_copy(
                 src_ref=source,
-                dst_ref=recv.at[kind, strip_at, parity],
-                send_sem=send_sem.at[kind + h, r, parity],
-                recv_sem=recv_sem.at[kind, r, parity],
+                dst_ref=recv.at[kind, strip_at, parity] if kind < 2 else recv.at[2, strip_at, parity, c],
+                send_sem=send_sem.at[kind + h, r, parity, c],
+                recv_sem=recv_sem.at[kind, r, parity, c],
                 device_id={"det": peer_det, "tm": turns[r][0], "pol": turns[r][1]},
                 device_id_type=MESH,
             )
 
-        def send_chunk(parity, h):
+        def send_chunk(parity, h, c):
             rows = pl.ds(pl.multiple_of(far[h] * strips * kept, strips * kept), strips * kept)
             return pltpu.make_async_remote_copy(
-                src_ref=spec_s.at[parity, :, rows, :],
-                dst_ref=passed.at[parity, h],
-                send_sem=chunk_send.at[parity, h],
-                recv_sem=chunk_recv.at[parity, h],
+                src_ref=spec_s.at[parity, c, rows, :],
+                dst_ref=passed.at[parity, h, c],
+                send_sem=chunk_send.at[parity, h, c],
+                recv_sem=chunk_recv.at[parity, h, c],
                 device_id={"det": near},
                 device_id_type=MESH,
             )
@@ -339,22 +339,23 @@
                 @pl.when(edge)
                 def _():
                     for h in range(2):
-                        send_chunk(parity, h).start()
+                        for c in range(2):
+                            send_chunk(parity, h, c).start()
     if not direct:
         return
 
     @pl.when(inner)
     def _():
         for parity in range(2):
-            for h in range(2):
-                send_chunk(parity, h).wait_recv()
+            for h, c in ((0, 0), (0, 1), (1, 0), (1, 1)):
+                send_chunk(parity, h, c).wait_recv()
                 rows = pl.ds(pl.multiple_of(far[h] * strips * kept, strips * kept), strips * kept)
-                both = passed[parity, h].astype(jnp.float32) + spec_s[parity, :, rows, :].astype(
-                    jnp.float32
-                )
-                joined[parity, h] = both.astype(jnp.bfloat16)
+                both = passed[parity, h, c].astype(jnp.float32) + spec_s[
+                    parity, c, rows, :
+                ].astype(jnp.float32)
+                joined[parity, h, c] = both.astype(jnp.bfloat16)
                 for r in range(strips):
-                    send(2, r, parity, h).start()
+                    send(2, r, parity, h, c).start()
 
     own = pl.ds(pl.multiple_of(me * kept, kept), kept)
     for parity in range(2):
@@ -362,7 +363,8 @@
     for parity in range(2):
         for kind in range(3):
             for r in range(0 if kind else 1, strips):
-                send(kind, r, parity).wait_recv()
+                for c in range(2 if kind == 2 else 1):
+                    send(kind, r, parity, 0, c).wait_recv()
         for strip in range(strips):
             total = recv[0, strip, parity].astype(jnp.float32)
             for kind in range(1, 3):
@@ -395,14 +397,16 @@
     def _():
         for parity in range(2):
             for h in range(2):
-                send_chunk(parity, h).wait_send()
+                for c in range(2):
+                    send_chunk(parity, h, c).wait_send()
 
     @pl.when(inner)
     def _():
         for parity in range(2):
             for h in range(2):
                 for r in range(strips):
-                    send(2, r, parity, h).wait_send()
+                    for c in range(2):
+                        send(2, r, parity, h, c).wait_send()
 
 
 def run_whole(sizes, direct, timestream, hwp_index, flags, pixel_index, tile_index, wafer, taps, angle):
@@ -441,10 +445,10 @@
             pltpu.VMEM((2, 2, 2, strips * kept, TILE), jnp.bfloat16),
             pltpu.VMEM((2, 2, 2, strips * kept, TILE), jnp.bfloat16),
             pltpu.VMEM((strips, 2, 2, kept, TILE), jnp.float32),
-            pltpu.SemaphoreType.DMA((4, strips, 2)),
-            pltpu.SemaphoreType.DMA((3, strips, 2)),
-            pltpu.SemaphoreType.DMA((2, 2)),
-            pltpu.SemaphoreType.DMA((2, 2)),
+            pltpu.SemaphoreType.DMA((4, strips, 2, 2)),
+            pltpu.SemaphoreType.DMA((3, strips, 2, 2)),
+            pltpu.SemaphoreType.DMA((2, 2, 2)),
+            pltpu.SemaphoreType.DMA((2, 2, 2)),
         ]
         out_shape, out_specs = jax.ShapeDtypeStruct((2, 2, kept, length), jnp.float32), vmem
     else:

time: 40.4 us -> 40.4 us (level)
  no operation moved by 1% of the time
where the time goes in v5:
time: 40.4 us; the launch traced here: 40.2 us
  Pallas kernels  37.8 us (94%)
  other arithmetic  1.8 us (4%)
  between operations  0.66 us (2%)
    pallas_call x1, Pallas kernels, run_whole(): pl.pallas_call(kernel, out_shape=out_shape, in_specs=[smem] * 3 + [hbm] *...  37.8 us
    sub x1, other arithmetic, body(): cosine * found[1] - sine * found[0]  1.78 us

profile of v5, /device:TPU:0, one launch (start us, length us, event | category | flops | bytes accessed | tf_op | source)
XLA Modules:
  0.0 40.2 jit_solution(4865420324781413499)
XLA Ops:
  0.7 37.8 %map_to_modes.1 = f32[2,2,32,512]{3,2,1,0:T(8,128)} custom-call(s32[8,16]{1,0:T(8,128)} %refs_0_.1, s32[8]{0:T(128)} %refs_1_.1, f32[8]{0:T(128)} %refs_2_.1, bf16[8,8192]{1,0:T(8,128)(2,1)} %refs_3_.1, s32[64,128]{1,0:T(8,128)} %bitcast.15, s32[8,8192]{1,0:T(8,128)} %refs_5_.1, s32[8,8192]{1,0:T(8,128)} %refs_6_.1, f32[7,33]{1,0:T(8,128)} %refs_7_.1, ...), custom_call_target="tpu_custom_call" | custom-call | tf_op jit(solution)/shard_map/map_to_modes/pallas_call | solution.py:460
  38.5 1.8 %fusion.1 = (f32[2,32,512]{2,1,0:T(8,128)}, f32[2,32,512]{2,1,0:T(8,128)}) fusion(f32[2,2,32,512]{3,2,1,0:T(8,128)} %map_to_modes.1, f32[32]{0:T(128)S(1)} %get-tuple-element.4, f32[32]{0:T(128)S(1)} %get-tuple-element.5, s32[512]{0:T(512)S(1)} %iota_add_fusion, pred[512]{0:T(512)(128)(4,1)S(1)} %iota_compare_fusion), kind=kLoop, calls=%fused_computation.3 | loop fusion | flops 491520 | bytes 527104 | tf_op jit(solution)/shard_map/sub | solution.py:552
  (3 shorter events, 0.0 us)
